TPU v7x, 32 devices: a whole 2x2x4 slice. The times are simulated.
32 devices in a mesh: layer: 16 (over z, x, core), row: 2 (over y).
Axes of the slice: x: 2, y: 2, z: 4, core: 2. Of those that a mesh axis runs over, the one named last changes fastest.
Arguments:
- coupling: bfloat16 [16, 1024, 1024], P('layer', 'row'), may hold values from -1 to 1, as said below
- band_off: int32 [16], P('layer'), may hold values from 0 to 32
- band_width: int32 [16], P('layer'), may hold values from 1 to 3
- incident: float32 [32, 1024], P(None, 'row'), may hold values from -6 to 6
- cotangent: float32 [32, 1024], P(None, 'row'), may hold values from -6 to 6
Outputs:
- transmitted: float32 [16, 32, 1024], P('layer', None, 'row')
- adjoint: float32 [16, 32, 1024], P('layer', None, 'row')
Inputs may be any that keep to these rules, and one draw needn't show every extreme that they name: coupling is antisymmetric in its last two dimensions.
All inputs are finite; a program needn't handle non-finite values.
Results may differ from a plain program's by a relative error of at most 0.012.
The roundings to bfloat16 on the way count: a program that leaves them out, or rounds other values in their place, can miss the bound.
Values may be sent and summed in bfloat16 or wider, within the bound.
No kernel may reach another device: no remote copies, remote signals or barrier semaphores. Data moves between devices by JAX's collectives and lax.ppermute only.
A program may use at most 64 MiB of HBM per device.

v0:
```python
import functools

import jax
import jax.numpy as jnp
from jax import lax
from jax.experimental import pallas as pl
from jax.experimental.pallas import tpu as pltpu
from jax.sharding import PartitionSpec as P

BLOCK = 16
GROUP = 8
LANES = 128
BLOCKS_PER_LANES = LANES // BLOCK
PACKED = LANES - BLOCK
DEGREE = 4
SMALL_GRANT = 4 * 1024 * 1024
CORES = 2


def fold_kernel(off_ref, width_ref, coupling_ref, folded_ref):
    rows, orders = coupling_ref.shape[1:]
    first = off_ref[0] - width_ref[0]
    last = off_ref[0] + width_ref[0]
    first_block = lax.axis_index("row") * (rows // BLOCK)
    lane = lax.broadcasted_iota(jnp.int32, (BLOCK, LANES), 1)
    sub = lax.broadcasted_iota(jnp.int32, (BLOCK, LANES), 0)
    top = orders // LANES - 1
    for local in range(rows // BLOCK):
        if local % BLOCKS_PER_LANES == 0:
            runs = []
        block = first_block + local
        start = (block + first) * BLOCK
        tile = start >> 7
        shift = start & (LANES - 1)
        here = slice(local * BLOCK, (local + 1) * BLOCK)

        def part(index):
            column = pl.multiple_of(jnp.clip(index, 0, top) * LANES, LANES)
            return coupling_ref[0, here, pl.ds(column, LANES)].astype(jnp.float32)

        near = lane >= shift
        column = jnp.where(near, lane, lane + LANES) + tile * LANES
        limit = jnp.minimum((block + last + 1) * BLOCK, orders)
        keep = (column > block * BLOCK + sub) & (column < limit)
        folded = jnp.where(keep, jnp.where(near, part(tile), part(tile + 1)), 0.0)
        is_last = block * BLOCK + sub == orders - 1
        folded = jnp.where(is_last, first.astype(jnp.float32), folded)
        runs.append(pltpu.roll(folded, (-first * BLOCK) & (LANES - 1), 1))
        if len(runs) == BLOCKS_PER_LANES:
            base = local * BLOCK // LANES * PACKED
            for b, run in enumerate(runs[:-1]):
                hole = lane // BLOCK == (b - 1) % BLOCKS_PER_LANES
                folded_ref[base + b * BLOCK : base + (b + 1) * BLOCK, :] = jnp.where(
                    hole, runs[-1], run
                ).astype(jnp.bfloat16)


def fold(coupling, band_off, band_width):
    rows, orders = coupling.shape[1:]
    smem = pl.BlockSpec(memory_space=pltpu.SMEM)
    vmem = pl.BlockSpec(memory_space=pltpu.VMEM)
    return pl.pallas_call(
        fold_kernel,
        out_shape=jax.ShapeDtypeStruct((rows // LANES * PACKED, LANES), jnp.bfloat16),
        in_specs=[smem, smem, vmem],
        out_specs=vmem,
        compiler_params=pltpu.CompilerParams(vmem_limit_bytes=SMALL_GRANT),
        name="fold",
    )(band_off, band_width, coupling)


def batch_kernel(*refs):
    rows = refs[-1].shape[1]
    for index, piece in enumerate(refs[:-1]):
        refs[-1][index] = piece[:rows, :]


def batch(pieces):
    vmem = pl.BlockSpec(memory_space=pltpu.VMEM)
    rows = min(piece.shape[0] for piece in pieces)
    return pl.pallas_call(
        batch_kernel,
        out_shape=jax.ShapeDtypeStruct((len(pieces), rows, LANES), pieces[0].dtype),
        in_specs=[vmem] * len(pieces),
        out_specs=vmem,
        compiler_params=pltpu.CompilerParams(vmem_limit_bytes=SMALL_GRANT),
        name="batch",
    )(*pieces)


def corner_kernel(folded, field, out):
    rows, panel = folded.shape[0], field.shape[1]
    count = field.shape[0]
    out[:rows, :] = folded[...]
    for u in range(panel // LANES):
        here = slice(rows + u * count, rows + (u + 1) * count)
        out[here, :] = field[:, u * LANES : (u + 1) * LANES].astype(jnp.bfloat16)


def corner(folded, field):
    vmem = pl.BlockSpec(memory_space=pltpu.VMEM)
    extra = field.size // LANES
    return pl.pallas_call(
        corner_kernel,
        out_shape=jax.ShapeDtypeStruct((folded.shape[0] + extra, LANES), folded.dtype),
        in_specs=[vmem] * 2,
        out_specs=vmem,
        compiler_params=pltpu.CompilerParams(vmem_limit_bytes=SMALL_GRANT),
        name="corner",
    )(folded, field)


def place(pieces, distances, folds):
    slot = lax.axis_index("layer") % GROUP
    row = lax.axis_index("row")
    rows = folds.shape[1] // lax.axis_size("row")
    for (ref, index), options in zip(pieces, distances):
        layer_mask, row_mask = by_core(options)
        here = pl.ds(pl.multiple_of((row ^ row_mask) * rows, BLOCK), rows)
        folds[slot ^ layer_mask, here, :] = ref[index, :rows, :]


def by_core(options):
    core = lax.axis_index("layer") % CORES
    return [jnp.where(core == 0, *pair) for pair in zip(*options)]


def place_field(own, others, field):
    row = lax.axis_index("row")
    count, panel = own.shape
    tiles = panel // LANES
    for u in range(tiles):
        field[row * tiles + u] = own[:, u * LANES : (u + 1) * LANES]
    for piece, row_mask in others:
        first = piece.shape[0] - tiles * count
        for u in range(tiles):
            here = slice(first + u * count, first + (u + 1) * count)
            field[(row ^ row_mask) * tiles + u] = piece[here, :].astype(jnp.float32)


def fill_masks(masks):
    row = lax.broadcasted_iota(jnp.int32, (LANES, LANES), 0)
    lane = lax.broadcasted_iota(jnp.int32, (LANES, LANES), 1)
    masks[0] = (lane >= row // BLOCK * BLOCK).astype(jnp.float32).astype(jnp.bfloat16)
    masks[1] = (row >= lane // BLOCK * BLOCK).astype(jnp.float32).astype(jnp.bfloat16)
    masks[2] = (row < LANES - 1).astype(jnp.float32).astype(jnp.bfloat16)
    own = lane // BLOCK != (row // BLOCK + BLOCKS_PER_LANES - 1) % BLOCKS_PER_LANES
    masks[3] = own.astype(jnp.float32).astype(jnp.bfloat16)


def expand(folds, slot, masks, upper, lower):
    tiles = upper.shape[0]
    lane = lax.broadcasted_iota(jnp.int32, (1, LANES), 1)
    eighth = folds[slot, (tiles - 1) * PACKED : (tiles - 1) * PACKED + BLOCK, :]
    last_row = eighth.astype(jnp.float32)[BLOCK - 1 :, :]
    last_row = jnp.where(lane >= PACKED, last_row, -float(LANES))
    first = jnp.max(last_row).astype(jnp.int32)
    for t in range(tiles):
        packed = folds[slot, t * PACKED : (t + 1) * PACKED, :]
        own = packed * masks[3, :PACKED, :]
        rest = packed - own
        eighth = [rest[b : b + BLOCK] for b in range(0, PACKED, BLOCK)]
        while len(eighth) > 1:
            eighth = [sum(eighth[i : i + 2][1:], eighth[i]) for i in range(0, len(eighth), 2)]
        run = jnp.concatenate([own, eighth[0]], axis=0)
        if t == tiles - 1:
            run = run * masks[2]
        near = run * masks[0]
        upper[t, :, :LANES] = near
        upper[t, :, LANES:] = run - near
        turned = run.T
        near = turned * masks[1]
        lower[t, :, :LANES] = near
        lower[(t + 1) % tiles, :, LANES:] = turned - near
    return first


def turn(parts, amount):
    step = 1
    while step < len(parts):
        moved = parts[step:] + parts[:step]
        there = amount & step != 0
        parts = [jnp.where(there, new, old) for new, old in zip(moved, parts)]
        step *= 2
    return parts


def banded_product(v, upper, lower, start):
    tiles = len(v)
    whole = start >> 3
    fine = (start & (BLOCKS_PER_LANES - 1)) * BLOCK
    lane = lax.broadcasted_iota(jnp.int32, v[0].shape, 1)
    turned = [pltpu.roll(part, (LANES - fine) & (LANES - 1), 1) for part in v]
    moved = turn(
        [
            jnp.where(lane < LANES - fine, turned[u], turned[(u + 1) % tiles])
            for u in range(tiles)
        ],
        whole,
    )
    first = [
        jnp.dot(v[t].astype(jnp.bfloat16), upper[t], preferred_element_type=jnp.float32)
        for t in range(tiles)
    ]
    second = [
        jnp.dot(moved[u].astype(jnp.bfloat16), lower[u], preferred_element_type=jnp.float32)
        for u in range(tiles)
    ]
    sums = [first[t][:, :LANES] + first[t - 1][:, LANES:] for t in range(tiles)]
    turned = [pltpu.roll(part, fine, 1) for part in sums]
    ahead = turn(
        [jnp.where(lane >= fine, turned[u], turned[u - 1]) for u in range(tiles)], -whole
    )
    return [
        ahead[u] - (second[u][:, :LANES] + second[(u + 1) % tiles][:, LANES:])
        for u in range(tiles)
    ]


def run_layer(x, sign, upper, lower, start):
    v = x
    for divisor in range(DEGREE, 0, -1):
        scale = sign * (1.0 / divisor)
        product = banded_product(v, upper, lower, start)
        v = [part + scale * term for part, term in zip(x, product)]
    return v


def cascade_first_kernel(distances, row_masks, *refs):
    pieces = []
    for count in distances[0]:
        pieces += [(refs[0], index) for index in range(count)]
        refs = refs[1:]
    others, refs = refs[: len(row_masks)], refs[len(row_masks) :]
    own, kept, upper, lower, starts, send, folds, masks, field = refs
    place(pieces, distances[1], folds)
    fill_masks(masks)
    place_field(own, list(zip(others, row_masks)), field)
    x = [field[u] for u in range(field.shape[0])]
    forward = lax.axis_index("layer") // GROUP == 0
    sign = jnp.where(forward, -1.0, 1.0)

    def prepare(k):
        slot = jnp.where(forward, k, GROUP - 1 - k)
        start = expand(folds, slot, masks, upper.at[k], lower.at[k])
        starts[k : k + 1, :] = jnp.full((1, LANES), start, jnp.int32)
        return start

    start = prepare(0)
    for k in range(GROUP):
        following = prepare(k + 1) if k + 1 < GROUP else None
        x = run_layer(x, sign, upper.at[k], lower.at[k], start)
        start = following
    mine = own_panel(x, kept.shape[-1])
    kept[0] = mine
    kept[1] = mine
    write_whole(x, send)


def cascade_next_kernel(step, groups, *refs):
    upper, lower, starts, field, before, kept, *send = refs
    panel = kept.shape[-1]
    group = lax.axis_index("layer") // GROUP
    forward = group == step
    backward = group == groups - 1 - step
    sign = jnp.where(forward, -1.0, 1.0)
    same_order = forward == (group == 0)
    x = field[...].astype(jnp.float32)
    x = [x[:, u : u + LANES] for u in range(0, x.shape[1], LANES)]

    order = [jnp.where(same_order, k, GROUP - 1 - k) for k in range(GROUP)]
    begin = [jnp.max(starts[pl.ds(at, 1), :]) for at in order]
    for at, start in zip(order, begin):
        x = run_layer(x, sign, upper.at[at], lower.at[at], start)
    mine = own_panel(x, panel)
    kept[0] = jnp.where(forward, mine, before[0])
    kept[1] = jnp.where(backward, mine, before[1])
    if send:
        write_whole(x, *send)


def write_whole(x, send):
    for u, part in enumerate(x):
        send[:, u * LANES : (u + 1) * LANES] = part.astype(jnp.bfloat16)


def own_panel(x, panel):
    row = lax.axis_index("row")
    tiles = panel // LANES
    mine = x[:tiles]
    for index in range(1, len(x) // tiles):
        there = x[index * tiles : (index + 1) * tiles]
        mine = [jnp.where(row == index, new, old) for new, old in zip(there, mine)]
    return jnp.concatenate(mine, axis=1)


def join_kernel(mine, theirs, *outs):
    core = lax.axis_index("layer") % CORES
    count = mine.shape[1]
    for kind, out in enumerate(outs):
        for part, at in ((mine, core), (theirs, 1 - core)):
            out[0, pl.ds(pl.multiple_of(at * count, count), count), :] = part[kind]


def join(mine, theirs):
    kinds, count, panel = mine.shape
    vmem = pl.BlockSpec(memory_space=pltpu.VMEM)
    return pl.pallas_call(
        join_kernel,
        out_shape=[jax.ShapeDtypeStruct((1, CORES * count, panel), mine.dtype)] * kinds,
        in_specs=[vmem] * 2,
        out_specs=[vmem] * kinds,
        compiler_params=pltpu.CompilerParams(vmem_limit_bytes=SMALL_GRANT),
        name="join",
    )(mine, theirs)


def run_first(batches, distances, others, row_masks, field, orders):
    count, panel = field.shape
    tiles = orders // LANES
    vmem = pl.BlockSpec(memory_space=pltpu.VMEM)
    window = jax.ShapeDtypeStruct((GROUP, tiles, LANES, 2 * LANES), jnp.bfloat16)
    return pl.pallas_call(
        functools.partial(cascade_first_kernel, distances, row_masks),
        out_shape=[
            jax.ShapeDtypeStruct((2, count, panel), jnp.float32),
            window,
            window,
            jax.ShapeDtypeStruct((GROUP, LANES), jnp.int32),
            jax.ShapeDtypeStruct((count, orders), jnp.bfloat16),
        ],
        in_specs=[vmem] * (len(batches) + len(others) + 1),
        out_specs=[vmem] * 5,
        scratch_shapes=[
            pltpu.VMEM((GROUP, tiles * PACKED, LANES), jnp.bfloat16),
            pltpu.VMEM((4, LANES, LANES), jnp.bfloat16),
            pltpu.VMEM((tiles, count, LANES), jnp.float32),
        ],
        compiler_params=pltpu.CompilerParams(vmem_limit_bytes=24 * 1024 * 1024),
        name="cascade_first",
    )(*batches, *others, field)


def run_next(step, groups, upper, lower, starts, field, kept):
    vmem = pl.BlockSpec(memory_space=pltpu.VMEM)
    out_shape = [jax.ShapeDtypeStruct(kept.shape, jnp.float32)]
    if step < groups - 1:
        out_shape.append(jax.ShapeDtypeStruct(field.shape, jnp.bfloat16))
    return pl.pallas_call(
        functools.partial(cascade_next_kernel, step, groups),
        out_shape=out_shape,
        in_specs=[vmem] * 5,
        out_specs=[vmem] * len(out_shape),
        compiler_params=pltpu.CompilerParams(vmem_limit_bytes=24 * 1024 * 1024),
        name=f"cascade_{step}",
    )(upper, lower, starts, field, kept)


def gather_batches(own, corner, across, rows):
    bits = [(0, 1 << b) for b in range(rows.bit_length() - 1)]
    bits += [(1 << b, 0) for b in range(1, GROUP.bit_length() - 1)]
    count = len(bits)

    def members(subset):
        return [b for b in range(count) if subset >> b & 1]

    def distance(subset):
        return tuple(
            tuple(sum(bits[(b + core) % count][axis] for b in members(subset)) for axis in (0, 1))
            for core in range(CORES)
        )

    subsets = sorted(range(1 << count), key=lambda m: (m.bit_count(), m))
    pieces = {0: own}
    for subset in subsets[1 : count + 1]:
        pieces[subset] = across(own, distance(subset))
    pieces[subsets[-1]] = across(corner, distance(subsets[-1]))
    for subset in subsets[count + 1 : -1]:
        which = members(subset)
        link = next((b for b in which if (b + 1) % count in which), which[0])
        pieces[subset] = across(pieces[subset ^ 1 << link], distance(1 << link))
    batches, counts, distances = [], [], []
    for part in (subsets[: count + 1], subsets[count + 1 :]):
        mine = batch([pieces[subset] for subset in part])
        batches += [mine, across(mine, ((1, 0), (1, 0)))]
        counts += [len(part), len(part)]
        distances += [distance(subset) for subset in part]
        distances += [
            tuple((a ^ 1, b) for a, b in options[::-1]) for options in distances[-len(part) :]
        ]
    return pieces[subsets[-1]], batches, (tuple(counts), tuple(distances))


def on_device(coupling, band_off, band_width, incident, cotangent):
    panel, orders = coupling.shape[1:]
    layers = lax.axis_size("layer")
    rows = lax.axis_size("row")
    groups = layers // GROUP

    def across(array, options):
        pairs = []
        for l in range(layers):
            layer_mask, row_mask = options[l % CORES]
            for r in range(rows):
                pairs.append((l * rows + r, (l ^ layer_mask) * rows + (r ^ row_mask)))
        return lax.ppermute(array, ("layer", "row"), pairs)

    folded = fold(coupling, band_off, band_width)
    layer = lax.axis_index("layer")
    share = incident.shape[0] // CORES
    folded, incident, cotangent = lax.optimization_barrier((folded, incident, cotangent))
    field = jnp.where(layer // GROUP == 0, incident, cotangent)
    field = lax.dynamic_slice_in_dim(field, layer % CORES * share, share)
    whole = corner(folded, field)
    from_corner, batches, distances = gather_batches(folded, whole, across, rows)
    others, row_masks = [from_corner], [rows - 1]
    for mask in range(1, rows - 1):
        others.append(across(whole, ((0, mask), (0, mask))))
        row_masks.append(mask)
    kept, upper, lower, starts, send = run_first(
        batches, distances, others, tuple(row_masks), field, orders
    )
    for step in range(1, groups):
        pairs = []
        for index in range(GROUP * rows):
            forward_from = (step - 1) * GROUP * rows + index
            adjoint_from = (groups - step) * GROUP * rows + index
            pairs.append((forward_from, forward_from + GROUP * rows))
            pairs.append((adjoint_from, adjoint_from - GROUP * rows))
        field = lax.ppermute(send, ("layer", "row"), pairs)
        kept, *send = run_next(step, groups, upper, lower, starts, field, kept)
        send = send[0] if send else None
    return tuple(join(kept, across(kept, ((1, 0), (1, 0)))))


def solution(mesh):
    in_specs = (P("layer", "row", None), P("layer"), P("layer"), P(None, "row"), P(None, "row"))
    out_specs = (P("layer", None, "row"), P("layer", None, "row"))
    return jax.shard_map(
        on_device, mesh=mesh, in_specs=in_specs, out_specs=out_specs, check_vma=False
    )
```

profile of v0, /device:TPU:0, one launch (start us, length us, event | category | flops | bytes accessed | tf_op | source)
XLA Modules:
  0.0 45.1 jit_solution(16278912522910749550)
XLA Ops:
  1.9 1.2 %copy-done = bf16[1,512,1024]{2,1,0:T(8,128)(2,1)S(1)} copy-done((bf16[1,512,1024]{2,1,0:T(8,128)(2,1)S(1)}, bf16[1,512,1024]{2,1,0:T(8,128)(2,1)}, u32[]{:S(2)}) %copy-start) | copy-done | bytes 1048600
  3.1 0.3 fold.1.refs_0_.folded
  3.5 3.1 %collective-permute-start.2 = (bf16[448,128]{1,0:T(8,128)(2,1)S(1)}, bf16[448,128]{1,0:T(8,128)(2,1)S(1)}, u32[]{:S(2)}, u32[]{:S(2)}) collective-permute-start(bf16[448,128]{1,0:T(8,128)(2,1)S(1)} %fold.1.refs_0_.folded), channel_id=1, source_target_pairs={{0,8},{1,9},{2,3},{3,2},{4,12},{5,13},{6,7},{7,6},{8,0},{9,1},{10,... | collective-permute-start | bytes 344072 | tf_op jit(solution)/shard_map/ppermute | solution.py:406
  6.6 1.5 %collective-permute-start.1 = (bf16[448,128]{1,0:T(8,128)(2,1)S(1)}, bf16[448,128]{1,0:T(8,128)(2,1)S(1)}, u32[]{:S(2)}, u32[]{:S(2)}) collective-permute-start(bf16[448,128]{1,0:T(8,128)(2,1)S(1)} %fold.1.refs_0_.folded), channel_id=1, source_target_pairs={{0,4},{1,5},{2,10},{3,11},{4,0},{5,1},{6,14},{7,15},{8,12},{9,13},... | collective-permute-start | bytes 344072 | tf_op jit(solution)/shard_map/ppermute | solution.py:406
  8.1 1.5 %collective-permute-start = (bf16[448,128]{1,0:T(8,128)(2,1)S(1)}, bf16[448,128]{1,0:T(8,128)(2,1)S(1)}, u32[]{:S(2)}, u32[]{:S(2)}) collective-permute-start(bf16[448,128]{1,0:T(8,128)(2,1)S(1)} %fold.1.refs_0_.folded), channel_id=1, source_target_pairs={{0,1},{1,0},{2,6},{3,7},{4,5},{5,4},{6,2},{7,3},{8,9},{9,8},{10,14... | collective-permute-start | bytes 344072 | tf_op jit(solution)/shard_map/ppermute | solution.py:406
  9.6 0.8 %dynamic-slice_select_fusion.field.refs_5_ = f32[16,512]{1,0:T(8,128)S(1)} fusion(f32[32,512]{1,0:T(8,128)} %param.9, s32[]{:T(128)S(6)} %select_n.26, f32[32,512]{1,0:T(8,128)} %param.8, pred[]{:T(512)S(6)} %eq.5), kind=kLoop, calls=%fused_computation | loop fusion | flops 8192 | bytes 98309 | tf_op jit(solution)/shard_map/jit(_where)/select_n | solution.py:412
  10.4 0.1 collective-permute-start.7
  10.5 1.9 %collective-permute-start.6 = (bf16[448,128]{1,0:T(8,128)(2,1)S(1)}, bf16[448,128]{1,0:T(8,128)(2,1)S(1)}, u32[]{:S(2)}, u32[]{:S(2)}) collective-permute-start(bf16[448,128]{1,0:T(8,128)(2,1)S(1)} %collective-permute-done.2.refs_3_), channel_id=1, source_target_pairs={{0,4},{1,5},{2,10},{3,11},{4,0},{5,1},{6,14},{7,15},{8,12},{9,13},... | collective-permute-start | bytes 344072 | tf_op jit(solution)/shard_map/ppermute | solution.py:406
  12.4 0.5 %collective-permute-done.1.refs_2_ = bf16[448,128]{1,0:T(8,128)(2,1)S(1)} collective-permute-done((bf16[448,128]{1,0:T(8,128)(2,1)S(1)}, bf16[448,128]{1,0:T(8,128)(2,1)S(1)}, u32[]{:S(2)}, u32[]{:S(2)}) %collective-permute-start.1) | collective-permute-done | bytes 114720 | tf_op jit(solution)/shard_map/ppermute | solution.py:406
  12.9 1.0 %collective-permute-start.4 = (bf16[448,128]{1,0:T(8,128)(2,1)S(1)}, bf16[448,128]{1,0:T(8,128)(2,1)S(1)}, u32[]{:S(2)}, u32[]{:S(2)}) collective-permute-start(bf16[448,128]{1,0:T(8,128)(2,1)S(1)} %collective-permute-done.1.refs_2_), channel_id=1, source_target_pairs={{0,1},{1,0},{2,6},{3,7},{4,5},{5,4},{6,2},{7,3},{8,9},{9,8},{10,14... | collective-permute-start | bytes 344072 | tf_op jit(solution)/shard_map/ppermute | solution.py:406
  13.8 1.6 %collective-permute-start.5 = (bf16[448,128]{1,0:T(8,128)(2,1)S(1)}, bf16[448,128]{1,0:T(8,128)(2,1)S(1)}, u32[]{:S(2)}, u32[]{:S(2)}) collective-permute-start(bf16[448,128]{1,0:T(8,128)(2,1)S(1)} %collective-permute-done.refs_1_), channel_id=1, source_target_pairs={{0,8},{1,9},{2,3},{3,2},{4,12},{5,13},{6,7},{7,6},{8,0},{9,1},{10,... | collective-permute-start | bytes 344072 | tf_op jit(solution)/shard_map/ppermute | solution.py:406
  15.4 0.1 collective-permute-start.3
  15.5 2.5 %collective-permute-done.7.refs_3_.refs_4_ = bf16[512,128]{1,0:T(8,128)(2,1)S(1)} collective-permute-done((bf16[512,128]{1,0:T(8,128)(2,1)S(1)}, bf16[512,128]{1,0:T(8,128)(2,1)S(1)}, u32[]{:S(2)}, u32[]{:S(2)}) %collective-permute-start.7) | collective-permute-done | bytes 131104 | tf_op jit(solution)/shard_map/ppermute | solution.py:406
  18.0 0.1 collective-permute-done.6.refs_2_
  18.1 1.0 %collective-permute-done.4.refs_0_ = bf16[448,128]{1,0:T(8,128)(2,1)S(1)} collective-permute-done((bf16[448,128]{1,0:T(8,128)(2,1)S(1)}, bf16[448,128]{1,0:T(8,128)(2,1)S(1)}, u32[]{:S(2)}, u32[]{:S(2)}) %collective-permute-start.4) | collective-permute-done | bytes 114720 | tf_op jit(solution)/shard_map/ppermute | solution.py:406
  19.2 0.1 collective-permute-start.8
  19.3 1.8 %collective-permute-done.8.refs_3_ = bf16[4,448,128]{2,1,0:T(8,128)(2,1)S(1)} collective-permute-done((bf16[4,448,128]{2,1,0:T(8,128)(2,1)S(1)}, bf16[4,448,128]{2,1,0:T(8,128)(2,1)S(1)}, u32[]{:S(2)}, u32[]{:S(2)}) %collective-permute-start.8) | collective-permute-done | bytes 458784 | tf_op jit(solution)/shard_map/ppermute | solution.py:406
  21.1 8.9 %cascade_first.1 = (f32[2,16,512]{2,1,0:T(8,128)S(1)}, bf16[8,8,128,256]{3,2,1,0:T(8,128)(2,1)S(1)}, bf16[8,8,128,256]{3,2,1,0:T(8,128)(2,1)S(1)}, s32[8,128]{1,0:T(8,128)S(1)}, bf16[16,1024]{1,0:T(8,128)(2,1)S(1)}) custom-call(bf16[4,448,128]{2,1,0:T(8,128)(2,1)S(1)} %batch.2.refs_0_, bf16[4,448,128]{2,1,0:T(8,128)(2,1)S(1)} %collective-permute-done.3.refs_1_, ...), custom_call_target="tpu_custom_call" | custom-call | tf_op jit(solution)/shard_map/cascade_first/pallas_call | solution.py:323
  29.9 2.7 %collective-permute-start.9 = (bf16[16,1024]{1,0:T(8,128)(2,1)S(1)}, bf16[16,1024]{1,0:T(8,128)(2,1)S(1)}, u32[]{:S(2)}, u32[]{:S(2)}) collective-permute-start(bf16[16,1024]{1,0:T(8,128)(2,1)S(1)} %get-tuple-element.16), channel_id=1, source_target_pairs={{0,16},{16,0},{1,17},{17,1},{2,18},{18,2},{3,19},{19,3},{4,20},{20... | collective-permute-start | bytes 98312 | tf_op jit(solution)/shard_map/ppermute | solution.py:430
  32.6 2.3 %collective-permute-done.9.refs_3_ = bf16[16,1024]{1,0:T(8,128)(2,1)S(1)} collective-permute-done((bf16[16,1024]{1,0:T(8,128)(2,1)S(1)}, bf16[16,1024]{1,0:T(8,128)(2,1)S(1)}, u32[]{:S(2)}, u32[]{:S(2)}) %collective-permute-start.9) | collective-permute-done | bytes 32800 | tf_op jit(solution)/shard_map/ppermute | solution.py:430
  34.9 8.2 %cascade_1.1.mine = f32[2,16,512]{2,1,0:T(8,128)S(1)} custom-call(bf16[8,8,128,256]{3,2,1,0:T(8,128)(2,1)S(1)} %get-tuple-element.13.refs_0_, bf16[8,8,128,256]{3,2,1,0:T(8,128)(2,1)S(1)} %get-tuple-element.14.refs_1_, s32[8,128]{1,0:T(8,128)S(1)} %get-tuple-element.15.refs_2_, bf16[16,1024]{1,0:T(8,128)(2,1)S(1)} %collective-permute-done.9.refs_3_, ...), custom_call_target="tpu_custom_call" | custom-call | tf_op jit(solution)/shard_map/cascade_1/pallas_call | solution.py:349
  43.1 0.1 collective-permute-start.10
  43.2 1.2 %collective-permute-done.10.theirs = f32[2,16,512]{2,1,0:T(8,128)S(1)} collective-permute-done((f32[2,16,512]{2,1,0:T(8,128)S(1)}, f32[2,16,512]{2,1,0:T(8,128)S(1)}, u32[]{:S(2)}, u32[]{:S(2)}) %collective-permute-start.10) | collective-permute-done | bytes 65568 | tf_op jit(solution)/shard_map/ppermute | solution.py:406
  44.4 0.7 %join.1 = (f32[1,32,512]{2,1,0:T(8,128)}, f32[1,32,512]{2,1,0:T(8,128)}) custom-call(f32[2,16,512]{2,1,0:T(8,128)S(1)} %cascade_1.1.mine, f32[2,16,512]{2,1,0:T(8,128)S(1)} %collective-permute-done.10.theirs), custom_call_target="tpu_custom_call" | custom-call | tf_op jit(solution)/shard_map/join/pallas_call | solution.py:308
  (8 shorter events, 0.1 us)
Async XLA Ops:
  1.9 1.2 %copy-start = (bf16[1,512,1024]{2,1,0:T(8,128)(2,1)S(1)}, bf16[1,512,1024]{2,1,0:T(8,128)(2,1)}, u32[]{:S(2)}) copy-start(bf16[1,512,1024]{2,1,0:T(8,128)(2,1)} %coupling_ref.1) | copy-start | bytes 3145732
  3.5 7.0 %collective-permute-start.2 = (bf16[448,128]{1,0:T(8,128)(2,1)S(1)}, bf16[448,128]{1,0:T(8,128)(2,1)S(1)}, u32[]{:S(2)}, u32[]{:S(2)}) collective-permute-start(bf16[448,128]{1,0:T(8,128)(2,1)S(1)} %fold.1.refs_0_.folded), channel_id=1, source_target_pairs={{0,8},{1,9},{2,3},{3,2},{4,12},{5,13},{6,7},{7,6},{8,0},{9,1},{10,... | collective-permute-start | bytes 344072 | tf_op jit(solution)/shard_map/ppermute | solution.py:406
  6.6 6.3 %collective-permute-start.1 = (bf16[448,128]{1,0:T(8,128)(2,1)S(1)}, bf16[448,128]{1,0:T(8,128)(2,1)S(1)}, u32[]{:S(2)}, u32[]{:S(2)}) collective-permute-start(bf16[448,128]{1,0:T(8,128)(2,1)S(1)} %fold.1.refs_0_.folded), channel_id=1, source_target_pairs={{0,4},{1,5},{2,10},{3,11},{4,0},{5,1},{6,14},{7,15},{8,12},{9,13},... | collective-permute-start | bytes 344072 | tf_op jit(solution)/shard_map/ppermute | solution.py:406
  8.1 5.8 %collective-permute-start = (bf16[448,128]{1,0:T(8,128)(2,1)S(1)}, bf16[448,128]{1,0:T(8,128)(2,1)S(1)}, u32[]{:S(2)}, u32[]{:S(2)}) collective-permute-start(bf16[448,128]{1,0:T(8,128)(2,1)S(1)} %fold.1.refs_0_.folded), channel_id=1, source_target_pairs={{0,1},{1,0},{2,6},{3,7},{4,5},{5,4},{6,2},{7,3},{8,9},{9,8},{10,14... | collective-permute-start | bytes 344072 | tf_op jit(solution)/shard_map/ppermute | solution.py:406
  10.4 7.6 %collective-permute-start.7 = (bf16[512,128]{1,0:T(8,128)(2,1)S(1)}, bf16[512,128]{1,0:T(8,128)(2,1)S(1)}, u32[]{:S(2)}, u32[]{:S(2)}) collective-permute-start(bf16[512,128]{1,0:T(8,128)(2,1)S(1)} %corner.1), channel_id=1, source_target_pairs={{0,13},{1,12},{2,15},{3,14},{4,9},{5,8},{6,11},{7,10},{8,5},{9,4},... | collective-permute-start | bytes 393224 | tf_op jit(solution)/shard_map/ppermute | solution.py:406
  10.5 7.7 %collective-permute-start.6 = (bf16[448,128]{1,0:T(8,128)(2,1)S(1)}, bf16[448,128]{1,0:T(8,128)(2,1)S(1)}, u32[]{:S(2)}, u32[]{:S(2)}) collective-permute-start(bf16[448,128]{1,0:T(8,128)(2,1)S(1)} %collective-permute-done.2.refs_3_), channel_id=1, source_target_pairs={{0,4},{1,5},{2,10},{3,11},{4,0},{5,1},{6,14},{7,15},{8,12},{9,13},... | collective-permute-start | bytes 344072 | tf_op jit(solution)/shard_map/ppermute | solution.py:406
  12.9 6.3 %collective-permute-start.4 = (bf16[448,128]{1,0:T(8,128)(2,1)S(1)}, bf16[448,128]{1,0:T(8,128)(2,1)S(1)}, u32[]{:S(2)}, u32[]{:S(2)}) collective-permute-start(bf16[448,128]{1,0:T(8,128)(2,1)S(1)} %collective-permute-done.1.refs_2_), channel_id=1, source_target_pairs={{0,1},{1,0},{2,6},{3,7},{4,5},{5,4},{6,2},{7,3},{8,9},{9,8},{10,14... | collective-permute-start | bytes 344072 | tf_op jit(solution)/shard_map/ppermute | solution.py:406
  13.8 5.3 %collective-permute-start.5 = (bf16[448,128]{1,0:T(8,128)(2,1)S(1)}, bf16[448,128]{1,0:T(8,128)(2,1)S(1)}, u32[]{:S(2)}, u32[]{:S(2)}) collective-permute-start(bf16[448,128]{1,0:T(8,128)(2,1)S(1)} %collective-permute-done.refs_1_), channel_id=1, source_target_pairs={{0,8},{1,9},{2,3},{3,2},{4,12},{5,13},{6,7},{7,6},{8,0},{9,1},{10,... | collective-permute-start | bytes 344072 | tf_op jit(solution)/shard_map/ppermute | solution.py:406
  15.4 3.8 %collective-permute-start.3 = (bf16[4,448,128]{2,1,0:T(8,128)(2,1)S(1)}, bf16[4,448,128]{2,1,0:T(8,128)(2,1)S(1)}, u32[]{:S(2)}, u32[]{:S(2)}) collective-permute-start(bf16[4,448,128]{2,1,0:T(8,128)(2,1)S(1)} %batch.2.refs_0_), channel_id=1, source_target_pairs={{0,2},{1,3},{2,0},{3,1},{4,6},{5,7},{6,4},{7,5},{8,10},{9,11},{10,... | collective-permute-start | bytes 1376264 | tf_op jit(solution)/shard_map/ppermute | solution.py:406
  19.2 1.9 %collective-permute-start.8 = (bf16[4,448,128]{2,1,0:T(8,128)(2,1)S(1)}, bf16[4,448,128]{2,1,0:T(8,128)(2,1)S(1)}, u32[]{:S(2)}, u32[]{:S(2)}) collective-permute-start(bf16[4,448,128]{2,1,0:T(8,128)(2,1)S(1)} %batch.3.refs_2_), channel_id=1, source_target_pairs={{0,2},{1,3},{2,0},{3,1},{4,6},{5,7},{6,4},{7,5},{8,10},{9,11},{10,... | collective-permute-start | bytes 1376264 | tf_op jit(solution)/shard_map/ppermute | solution.py:406
  29.9 5.0 %collective-permute-start.9 = (bf16[16,1024]{1,0:T(8,128)(2,1)S(1)}, bf16[16,1024]{1,0:T(8,128)(2,1)S(1)}, u32[]{:S(2)}, u32[]{:S(2)}) collective-permute-start(bf16[16,1024]{1,0:T(8,128)(2,1)S(1)} %get-tuple-element.16), channel_id=1, source_target_pairs={{0,16},{16,0},{1,17},{17,1},{2,18},{18,2},{3,19},{19,3},{4,20},{20... | collective-permute-start | bytes 98312 | tf_op jit(solution)/shard_map/ppermute | solution.py:430
  43.1 1.3 %collective-permute-start.10 = (f32[2,16,512]{2,1,0:T(8,128)S(1)}, f32[2,16,512]{2,1,0:T(8,128)S(1)}, u32[]{:S(2)}, u32[]{:S(2)}) collective-permute-start(f32[2,16,512]{2,1,0:T(8,128)S(1)} %cascade_1.1.mine), channel_id=1, source_target_pairs={{0,2},{1,3},{2,0},{3,1},{4,6},{5,7},{6,4},{7,5},{8,10},{9,11},{10,... | collective-permute-start | bytes 196616 | tf_op jit(solution)/shard_map/ppermute | solution.py:406
where the time goes:
time: 45.3 us; the launch traced here: 45.1 us
  Pallas kernels  18.1 us (40%)
  starting transfers between devices  13.5 us (30%)
  waiting for transfers between devices  9.45 us (21%)
  between operations  2.01 us (4%)
  local copies, waits for them, and re-layouts  1.22 us (3%)
  other arithmetic  0.78 us (2%)
    ppermute x10, starting transfers between devices, across(): return lax.ppermute(array, ('layer', 'row'), pairs)  10.8 us
    pallas_call x1, Pallas kernels, run_first(): pl.pallas_call(functools.partial(cascade_first_kernel, distances, row_mas...  8.85 us
    pallas_call x1, Pallas kernels, run_next(): pl.pallas_call(functools.partial(cascade_next_kernel, step, groups), out_...  8.19 us
    ppermute x10, waiting for transfers between devices, across(): return lax.ppermute(array, ('layer', 'row'), pairs)  7.14 us
    ppermute x1, starting transfers between devices, on_device(): field = lax.ppermute(send, ('layer', 'row'), pairs)  2.66 us
    ppermute x1, waiting for transfers between devices, on_device(): field = lax.ppermute(send, ('layer', 'row'), pairs)  2.31 us
    unnamed x2, local copies, waits for them, and re-layouts  1.22 us
  transfers between devices with their start and end apart: 11, of which 7 were waited for; matrix products, arithmetic and copies ran while one was open for 2% of the time, Pallas kernels for 0%

commit v1 on v0

--- a/solution.py
+++ b/solution.py
@@ -88,28 +88,6 @@
     )(*pieces)
 
 
-def corner_kernel(folded, field, out):
-    rows, panel = folded.shape[0], field.shape[1]
-    count = field.shape[0]
-    out[:rows, :] = folded[...]
-    for u in range(panel // LANES):
-        here = slice(rows + u * count, rows + (u + 1) * count)
-        out[here, :] = field[:, u * LANES : (u + 1) * LANES].astype(jnp.bfloat16)
-
-
-def corner(folded, field):
-    vmem = pl.BlockSpec(memory_space=pltpu.VMEM)
-    extra = field.size // LANES
-    return pl.pallas_call(
-        corner_kernel,
-        out_shape=jax.ShapeDtypeStruct((folded.shape[0] + extra, LANES), folded.dtype),
-        in_specs=[vmem] * 2,
-        out_specs=vmem,
-        compiler_params=pltpu.CompilerParams(vmem_limit_bytes=SMALL_GRANT),
-        name="corner",
-    )(folded, field)
-
-
 def place(pieces, distances, folds):
     slot = lax.axis_index("layer") % GROUP
     row = lax.axis_index("row")
@@ -127,15 +105,10 @@
 
 def place_field(own, others, field):
     row = lax.axis_index("row")
-    count, panel = own.shape
-    tiles = panel // LANES
-    for u in range(tiles):
-        field[row * tiles + u] = own[:, u * LANES : (u + 1) * LANES]
-    for piece, row_mask in others:
-        first = piece.shape[0] - tiles * count
+    tiles = own.shape[1] // LANES
+    for part, row_mask in [(own, 0), *others]:
         for u in range(tiles):
-            here = slice(first + u * count, first + (u + 1) * count)
-            field[(row ^ row_mask) * tiles + u] = piece[here, :].astype(jnp.float32)
+            field[(row ^ row_mask) * tiles + u] = part[:, u * LANES : (u + 1) * LANES]
 
 
 def fill_masks(masks):
@@ -226,16 +199,16 @@
     return v
 
 
-def cascade_first_kernel(distances, row_masks, *refs):
+def cascade_first_kernel(distances, shares, *refs):
     pieces = []
     for count in distances[0]:
         pieces += [(refs[0], index) for index in range(count)]
         refs = refs[1:]
-    others, refs = refs[: len(row_masks)], refs[len(row_masks) :]
-    own, kept, upper, lower, starts, send, folds, masks, field = refs
+    (own, *others), refs = refs[:shares], refs[shares:]
+    kept, upper, lower, starts, send, folds, masks, field = refs
     place(pieces, distances[1], folds)
     fill_masks(masks)
-    place_field(own, list(zip(others, row_masks)), field)
+    place_field(own, [(part, n + 1) for n, part in enumerate(others)], field)
     x = [field[u] for u in range(field.shape[0])]
     forward = lax.axis_index("layer") // GROUP == 0
     sign = jnp.where(forward, -1.0, 1.0)
@@ -315,13 +288,13 @@
     )(mine, theirs)
 
 
-def run_first(batches, distances, others, row_masks, field, orders):
-    count, panel = field.shape
+def run_first(batches, distances, fields, orders):
+    count, panel = fields[0].shape
     tiles = orders // LANES
     vmem = pl.BlockSpec(memory_space=pltpu.VMEM)
     window = jax.ShapeDtypeStruct((GROUP, tiles, LANES, 2 * LANES), jnp.bfloat16)
     return pl.pallas_call(
-        functools.partial(cascade_first_kernel, distances, row_masks),
+        functools.partial(cascade_first_kernel, distances, len(fields)),
         out_shape=[
             jax.ShapeDtypeStruct((2, count, panel), jnp.float32),
             window,
@@ -329,7 +302,7 @@
             jax.ShapeDtypeStruct((GROUP, LANES), jnp.int32),
             jax.ShapeDtypeStruct((count, orders), jnp.bfloat16),
         ],
-        in_specs=[vmem] * (len(batches) + len(others) + 1),
+        in_specs=[vmem] * (len(batches) + len(fields)),
         out_specs=[vmem] * 5,
         scratch_shapes=[
             pltpu.VMEM((GROUP, tiles * PACKED, LANES), jnp.bfloat16),
@@ -338,7 +311,7 @@
         ],
         compiler_params=pltpu.CompilerParams(vmem_limit_bytes=24 * 1024 * 1024),
         name="cascade_first",
-    )(*batches, *others, field)
+    )(*batches, *fields)
 
 
 def run_next(step, groups, upper, lower, starts, field, kept):
@@ -356,7 +329,7 @@
     )(upper, lower, starts, field, kept)
 
 
-def gather_batches(own, corner, across, rows):
+def gather_batches(own, start_fields, across, rows):
     bits = [(0, 1 << b) for b in range(rows.bit_length() - 1)]
     bits += [(1 << b, 0) for b in range(1, GROUP.bit_length() - 1)]
     count = len(bits)
@@ -372,14 +345,15 @@
 
     subsets = sorted(range(1 << count), key=lambda m: (m.bit_count(), m))
     pieces = {0: own}
-    for subset in subsets[1 : count + 1]:
+    for subset in subsets[1 : count + 1] + subsets[-1:]:
         pieces[subset] = across(own, distance(subset))
-    pieces[subsets[-1]] = across(corner, distance(subsets[-1]))
     for subset in subsets[count + 1 : -1]:
         which = members(subset)
         link = next((b for b in which if (b + 1) % count in which), which[0])
         pieces[subset] = across(pieces[subset ^ 1 << link], distance(1 << link))
     batches, counts, distances = [], [], []
+    pieces[subsets[count]], fields = start_fields(pieces[subsets[count]])
+    fields, pieces[subsets[-1]] = lax.optimization_barrier((fields, pieces[subsets[-1]]))
     for part in (subsets[: count + 1], subsets[count + 1 :]):
         mine = batch([pieces[subset] for subset in part])
         batches += [mine, across(mine, ((1, 0), (1, 0)))]
@@ -388,7 +362,7 @@
         distances += [
             tuple((a ^ 1, b) for a, b in options[::-1]) for options in distances[-len(part) :]
         ]
-    return pieces[subsets[-1]], batches, (tuple(counts), tuple(distances))
+    return fields, batches, (tuple(counts), tuple(distances))
 
 
 def on_device(coupling, band_off, band_width, incident, cotangent):
@@ -408,18 +382,17 @@
     folded = fold(coupling, band_off, band_width)
     layer = lax.axis_index("layer")
     share = incident.shape[0] // CORES
-    folded, incident, cotangent = lax.optimization_barrier((folded, incident, cotangent))
-    field = jnp.where(layer // GROUP == 0, incident, cotangent)
-    field = lax.dynamic_slice_in_dim(field, layer % CORES * share, share)
-    whole = corner(folded, field)
-    from_corner, batches, distances = gather_batches(folded, whole, across, rows)
-    others, row_masks = [from_corner], [rows - 1]
-    for mask in range(1, rows - 1):
-        others.append(across(whole, ((0, mask), (0, mask))))
-        row_masks.append(mask)
-    kept, upper, lower, starts, send = run_first(
-        batches, distances, others, tuple(row_masks), field, orders
-    )
+
+    def start_fields(after):
+        after, first, last = lax.optimization_barrier((after, incident, cotangent))
+        layer = lax.axis_index("layer")
+        share = incident.shape[0] // CORES
+        own = jnp.where(layer // GROUP == 0, first, last)
+        own = lax.dynamic_slice_in_dim(own, layer % CORES * share, share)
+        return after, [own] + [across(own, ((0, m), (0, m))) for m in range(1, rows)]
+
+    fields, batches, distances = gather_batches(folded, start_fields, across, rows)
+    kept, upper, lower, starts, send = run_first(batches, distances, fields, orders)
     for step in range(1, groups):
         pairs = []
         for index in range(GROUP * rows):

time: 45.3 us -> 46.3 us (1.022)
  waiting for transfers between devices: 9.45 us -> 10.5 us
    ppermute x10 -> x11, waiting for transfers between devices: 7.14 us -> 7.91 us  [across(): return lax.ppermute(array, ('layer', 'row'), pairs)]
    ppermute x10 -> x11, starting transfers between devices: 10.8 us -> 10.9 us  [across(): return lax.ppermute(array, ('layer', 'row'), pairs)]
    pallas_call x2 -> x1, Pallas kernels: 8.86 us -> 8.84 us  [run_first(): pl.pallas_call(functools.partial(cascade_first_kernel, distances, len(fie...]
  transfers between devices with their start and end apart: 11 -> 12, of which waited for: 7 -> 6; matrix products, arithmetic and copies ran while one was open for 2% -> 2% of each run, Pallas kernels for 0% -> 0%
where the time goes in v1:
time: 46.3 us; the launch traced here: 46.1 us
  Pallas kernels  18.1 us (39%)
  starting transfers between devices  13.5 us (29%)
  waiting for transfers between devices  10.5 us (23%)
  between operations  2 us (4%)
  local copies, waits for them, and re-layouts  1.22 us (3%)
  other arithmetic  0.78 us (2%)
    ppermute x11, starting transfers between devices, across(): return lax.ppermute(array, ('layer', 'row'), pairs)  10.9 us
    pallas_call x1, Pallas kernels, run_first(): pl.pallas_call(functools.partial(cascade_first_kernel, distances, len(fie...  8.84 us
    pallas_call x1, Pallas kernels, run_next(): pl.pallas_call(functools.partial(cascade_next_kernel, step, groups), out_...  8.19 us
    ppermute x11, waiting for transfers between devices, across(): return lax.ppermute(array, ('layer', 'row'), pairs)  7.91 us
    ppermute x1, starting transfers between devices, on_device(): field = lax.ppermute(send, ('layer', 'row'), pairs)  2.66 us
    ppermute x1, waiting for transfers between devices, on_device(): field = lax.ppermute(send, ('layer', 'row'), pairs)  2.57 us
    unnamed x2, local copies, waits for them, and re-layouts  1.22 us
  transfers between devices with their start and end apart: 12, of which 6 were waited for; matrix products, arithmetic and copies ran while one was open for 2% of the time, Pallas kernels for 0%

profile of v1, /device:TPU:0, one launch (start us, length us, event | category | flops | bytes accessed | tf_op | source)
XLA Modules:
  0.0 46.1 jit_solution(10489214905415072521)
XLA Ops:
  1.9 1.2 %copy-done = bf16[1,512,1024]{2,1,0:T(8,128)(2,1)S(1)} copy-done((bf16[1,512,1024]{2,1,0:T(8,128)(2,1)S(1)}, bf16[1,512,1024]{2,1,0:T(8,128)(2,1)}, u32[]{:S(2)}) %copy-start) | copy-done | bytes 1048600
  3.1 0.3 fold.1.refs_0_
  3.5 3.1 %collective-permute-start.2 = (bf16[448,128]{1,0:T(8,128)(2,1)S(1)}, bf16[448,128]{1,0:T(8,128)(2,1)S(1)}, u32[]{:S(2)}, u32[]{:S(2)}) collective-permute-start(bf16[448,128]{1,0:T(8,128)(2,1)S(1)} %fold.1.refs_0_), channel_id=1, source_target_pairs={{0,8},{1,9},{2,3},{3,2},{4,12},{5,13},{6,7},{7,6},{8,0},{9,1},{10,... | collective-permute-start | bytes 344072 | tf_op jit(solution)/shard_map/ppermute | solution.py:380
  6.6 1.5 %collective-permute-start.1 = (bf16[448,128]{1,0:T(8,128)(2,1)S(1)}, bf16[448,128]{1,0:T(8,128)(2,1)S(1)}, u32[]{:S(2)}, u32[]{:S(2)}) collective-permute-start(bf16[448,128]{1,0:T(8,128)(2,1)S(1)} %fold.1.refs_0_), channel_id=1, source_target_pairs={{0,4},{1,5},{2,10},{3,11},{4,0},{5,1},{6,14},{7,15},{8,12},{9,13},... | collective-permute-start | bytes 344072 | tf_op jit(solution)/shard_map/ppermute | solution.py:380
  8.1 1.5 %collective-permute-start = (bf16[448,128]{1,0:T(8,128)(2,1)S(1)}, bf16[448,128]{1,0:T(8,128)(2,1)S(1)}, u32[]{:S(2)}, u32[]{:S(2)}) collective-permute-start(bf16[448,128]{1,0:T(8,128)(2,1)S(1)} %fold.1.refs_0_), channel_id=1, source_target_pairs={{0,1},{1,0},{2,6},{3,7},{4,5},{5,4},{6,2},{7,3},{8,9},{9,8},{10,14... | collective-permute-start | bytes 344072 | tf_op jit(solution)/shard_map/ppermute | solution.py:380
  9.6 0.5 %collective-permute-done.2.refs_3_ = bf16[448,128]{1,0:T(8,128)(2,1)S(1)} collective-permute-done((bf16[448,128]{1,0:T(8,128)(2,1)S(1)}, bf16[448,128]{1,0:T(8,128)(2,1)S(1)}, u32[]{:S(2)}, u32[]{:S(2)}) %collective-permute-start.2) | collective-permute-done | bytes 114720 | tf_op jit(solution)/shard_map/ppermute | solution.py:380
  10.1 2.3 %collective-permute-start.6 = (bf16[448,128]{1,0:T(8,128)(2,1)S(1)}, bf16[448,128]{1,0:T(8,128)(2,1)S(1)}, u32[]{:S(2)}, u32[]{:S(2)}) collective-permute-start(bf16[448,128]{1,0:T(8,128)(2,1)S(1)} %collective-permute-done.2.refs_3_), channel_id=1, source_target_pairs={{0,4},{1,5},{2,10},{3,11},{4,0},{5,1},{6,14},{7,15},{8,12},{9,13},... | collective-permute-start | bytes 344072 | tf_op jit(solution)/shard_map/ppermute | solution.py:380
  12.4 1.4 %collective-permute-done.1.refs_2_ = bf16[448,128]{1,0:T(8,128)(2,1)S(1)} collective-permute-done((bf16[448,128]{1,0:T(8,128)(2,1)S(1)}, bf16[448,128]{1,0:T(8,128)(2,1)S(1)}, u32[]{:S(2)}, u32[]{:S(2)}) %collective-permute-start.1) | collective-permute-done | bytes 114720 | tf_op jit(solution)/shard_map/ppermute | solution.py:380
  13.7 0.0 collective-permute-start.4
  13.7 0.0 collective-permute-done.refs_1_
  13.7 1.0 %collective-permute-start.5 = (bf16[448,128]{1,0:T(8,128)(2,1)S(1)}, bf16[448,128]{1,0:T(8,128)(2,1)S(1)}, u32[]{:S(2)}, u32[]{:S(2)}) collective-permute-start(bf16[448,128]{1,0:T(8,128)(2,1)S(1)} %collective-permute-done.refs_1_), channel_id=1, source_target_pairs={{0,8},{1,9},{2,3},{3,2},{4,12},{5,13},{6,7},{7,6},{8,0},{9,1},{10,... | collective-permute-start | bytes 344072 | tf_op jit(solution)/shard_map/ppermute | solution.py:380
  14.8 0.8 %dynamic-slice_select_fusion.refs_4_ = f32[16,512]{1,0:T(8,128)S(1)} fusion(f32[32,512]{1,0:T(8,128)} %param.9, s32[]{:T(128)S(6)} %select_n.26, f32[32,512]{1,0:T(8,128)} %param.8, pred[]{:T(512)S(6)} %eq.5), kind=kLoop, calls=%fused_computation | loop fusion | flops 8192 | bytes 98309 | tf_op jit(solution)/shard_map/jit(_where)/select_n | solution.py:390
  15.6 1.2 %collective-permute-start.7 = (f32[16,512]{1,0:T(8,128)S(1)}, f32[16,512]{1,0:T(8,128)S(1)}, u32[]{:S(2)}, u32[]{:S(2)}) collective-permute-start(f32[16,512]{1,0:T(8,128)S(1)} %dynamic-slice_select_fusion.refs_4_), channel_id=1, source_target_pairs={{0,1},{1,0},{2,3},{3,2},{4,5},{5,4},{6,7},{7,6},{8,9},{9,8},{10,11... | collective-permute-start | bytes 98312 | tf_op jit(solution)/shard_map/ppermute | solution.py:380
  16.8 0.1 collective-permute-start.3
  16.9 3.0 %collective-permute-done.7.refs_5_ = f32[16,512]{1,0:T(8,128)S(1)} collective-permute-done((f32[16,512]{1,0:T(8,128)S(1)}, f32[16,512]{1,0:T(8,128)S(1)}, u32[]{:S(2)}, u32[]{:S(2)}) %collective-permute-start.7) | collective-permute-done | bytes 32800 | tf_op jit(solution)/shard_map/ppermute | solution.py:380
  20.0 0.1 collective-permute-start.9
  20.0 1.8 %collective-permute-done.9.refs_3_ = bf16[4,448,128]{2,1,0:T(8,128)(2,1)S(1)} collective-permute-done((bf16[4,448,128]{2,1,0:T(8,128)(2,1)S(1)}, bf16[4,448,128]{2,1,0:T(8,128)(2,1)S(1)}, u32[]{:S(2)}, u32[]{:S(2)}) %collective-permute-start.9) | collective-permute-done | bytes 458784 | tf_op jit(solution)/shard_map/ppermute | solution.py:380
  21.8 8.8 %cascade_first.1 = (f32[2,16,512]{2,1,0:T(8,128)S(1)}, bf16[8,8,128,256]{3,2,1,0:T(8,128)(2,1)S(1)}, bf16[8,8,128,256]{3,2,1,0:T(8,128)(2,1)S(1)}, s32[8,128]{1,0:T(8,128)S(1)}, bf16[16,1024]{1,0:T(8,128)(2,1)S(1)}) custom-call(bf16[4,448,128]{2,1,0:T(8,128)(2,1)S(1)} %batch.2.refs_0_, bf16[4,448,128]{2,1,0:T(8,128)(2,1)S(1)} %collective-permute-done.3.refs_1_, ...), custom_call_target="tpu_custom_call" | custom-call | tf_op jit(solution)/shard_map/cascade_first/pallas_call | solution.py:296
  30.7 2.7 %collective-permute-start.10 = (bf16[16,1024]{1,0:T(8,128)(2,1)S(1)}, bf16[16,1024]{1,0:T(8,128)(2,1)S(1)}, u32[]{:S(2)}, u32[]{:S(2)}) collective-permute-start(bf16[16,1024]{1,0:T(8,128)(2,1)S(1)} %get-tuple-element.22), channel_id=1, source_target_pairs={{0,16},{16,0},{1,17},{17,1},{2,18},{18,2},{3,19},{19,3},{4,20},{20... | collective-permute-start | bytes 98312 | tf_op jit(solution)/shard_map/ppermute | solution.py:403
  33.3 2.6 %collective-permute-done.10.refs_3_ = bf16[16,1024]{1,0:T(8,128)(2,1)S(1)} collective-permute-done((bf16[16,1024]{1,0:T(8,128)(2,1)S(1)}, bf16[16,1024]{1,0:T(8,128)(2,1)S(1)}, u32[]{:S(2)}, u32[]{:S(2)}) %collective-permute-start.10) | collective-permute-done | bytes 32800 | tf_op jit(solution)/shard_map/ppermute | solution.py:403
  35.9 8.2 %cascade_1.1.mine = f32[2,16,512]{2,1,0:T(8,128)S(1)} custom-call(bf16[8,8,128,256]{3,2,1,0:T(8,128)(2,1)S(1)} %get-tuple-element.19.refs_0_, bf16[8,8,128,256]{3,2,1,0:T(8,128)(2,1)S(1)} %get-tuple-element.20.refs_1_, s32[8,128]{1,0:T(8,128)S(1)} %get-tuple-element.21.refs_2_, bf16[16,1024]{1,0:T(8,128)(2,1)S(1)} %collective-permute-done.10.refs_3_, ...), custom_call_target="tpu_custom_call" | custom-call | tf_op jit(solution)/shard_map/cascade_1/pallas_call | solution.py:322
  44.1 0.1 collective-permute-start.11
  44.2 1.2 %collective-permute-done.11.theirs = f32[2,16,512]{2,1,0:T(8,128)S(1)} collective-permute-done((f32[2,16,512]{2,1,0:T(8,128)S(1)}, f32[2,16,512]{2,1,0:T(8,128)S(1)}, u32[]{:S(2)}, u32[]{:S(2)}) %collective-permute-start.11) | collective-permute-done | bytes 65568 | tf_op jit(solution)/shard_map/ppermute | solution.py:380
  45.4 0.7 %join.1 = (f32[1,32,512]{2,1,0:T(8,128)}, f32[1,32,512]{2,1,0:T(8,128)}) custom-call(f32[2,16,512]{2,1,0:T(8,128)S(1)} %cascade_1.1.mine, f32[2,16,512]{2,1,0:T(8,128)S(1)} %collective-permute-done.11.theirs), custom_call_target="tpu_custom_call" | custom-call | tf_op jit(solution)/shard_map/join/pallas_call | solution.py:281
  (9 shorter events, 0.1 us)
Async XLA Ops:
  1.9 1.2 %copy-start = (bf16[1,512,1024]{2,1,0:T(8,128)(2,1)S(1)}, bf16[1,512,1024]{2,1,0:T(8,128)(2,1)}, u32[]{:S(2)}) copy-start(bf16[1,512,1024]{2,1,0:T(8,128)(2,1)} %coupling_ref.1) | copy-start | bytes 3145732
  3.5 6.6 %collective-permute-start.2 = (bf16[448,128]{1,0:T(8,128)(2,1)S(1)}, bf16[448,128]{1,0:T(8,128)(2,1)S(1)}, u32[]{:S(2)}, u32[]{:S(2)}) collective-permute-start(bf16[448,128]{1,0:T(8,128)(2,1)S(1)} %fold.1.refs_0_), channel_id=1, source_target_pairs={{0,8},{1,9},{2,3},{3,2},{4,12},{5,13},{6,7},{7,6},{8,0},{9,1},{10,... | collective-permute-start | bytes 344072 | tf_op jit(solution)/shard_map/ppermute | solution.py:380
  6.6 7.2 %collective-permute-start.1 = (bf16[448,128]{1,0:T(8,128)(2,1)S(1)}, bf16[448,128]{1,0:T(8,128)(2,1)S(1)}, u32[]{:S(2)}, u32[]{:S(2)}) collective-permute-start(bf16[448,128]{1,0:T(8,128)(2,1)S(1)} %fold.1.refs_0_), channel_id=1, source_target_pairs={{0,4},{1,5},{2,10},{3,11},{4,0},{5,1},{6,14},{7,15},{8,12},{9,13},... | collective-permute-start | bytes 344072 | tf_op jit(solution)/shard_map/ppermute | solution.py:380
  8.1 5.7 %collective-permute-start = (bf16[448,128]{1,0:T(8,128)(2,1)S(1)}, bf16[448,128]{1,0:T(8,128)(2,1)S(1)}, u32[]{:S(2)}, u32[]{:S(2)}) collective-permute-start(bf16[448,128]{1,0:T(8,128)(2,1)S(1)} %fold.1.refs_0_), channel_id=1, source_target_pairs={{0,1},{1,0},{2,6},{3,7},{4,5},{5,4},{6,2},{7,3},{8,9},{9,8},{10,14... | collective-permute-start | bytes 344072 | tf_op jit(solution)/shard_map/ppermute | solution.py:380
  9.6 7.2 %collective-permute-start.8 = (bf16[448,128]{1,0:T(8,128)(2,1)S(1)}, bf16[448,128]{1,0:T(8,128)(2,1)S(1)}, u32[]{:S(2)}, u32[]{:S(2)}) collective-permute-start(bf16[448,128]{1,0:T(8,128)(2,1)S(1)} %fold.1.refs_0_), channel_id=1, source_target_pairs={{0,13},{1,12},{2,15},{3,14},{4,9},{5,8},{6,11},{7,10},{8,5},{9,4},... | collective-permute-start | bytes 344072 | tf_op jit(solution)/shard_map/ppermute | solution.py:380
  10.1 9.8 %collective-permute-start.6 = (bf16[448,128]{1,0:T(8,128)(2,1)S(1)}, bf16[448,128]{1,0:T(8,128)(2,1)S(1)}, u32[]{:S(2)}, u32[]{:S(2)}) collective-permute-start(bf16[448,128]{1,0:T(8,128)(2,1)S(1)} %collective-permute-done.2.refs_3_), channel_id=1, source_target_pairs={{0,4},{1,5},{2,10},{3,11},{4,0},{5,1},{6,14},{7,15},{8,12},{9,13},... | collective-permute-start | bytes 344072 | tf_op jit(solution)/shard_map/ppermute | solution.py:380
  13.7 6.2 %collective-permute-start.4 = (bf16[448,128]{1,0:T(8,128)(2,1)S(1)}, bf16[448,128]{1,0:T(8,128)(2,1)S(1)}, u32[]{:S(2)}, u32[]{:S(2)}) collective-permute-start(bf16[448,128]{1,0:T(8,128)(2,1)S(1)} %collective-permute-done.1.refs_2_), channel_id=1, source_target_pairs={{0,1},{1,0},{2,6},{3,7},{4,5},{5,4},{6,2},{7,3},{8,9},{9,8},{10,14... | collective-permute-start | bytes 344072 | tf_op jit(solution)/shard_map/ppermute | solution.py:380
  13.7 6.2 %collective-permute-start.5 = (bf16[448,128]{1,0:T(8,128)(2,1)S(1)}, bf16[448,128]{1,0:T(8,128)(2,1)S(1)}, u32[]{:S(2)}, u32[]{:S(2)}) collective-permute-start(bf16[448,128]{1,0:T(8,128)(2,1)S(1)} %collective-permute-done.refs_1_), channel_id=1, source_target_pairs={{0,8},{1,9},{2,3},{3,2},{4,12},{5,13},{6,7},{7,6},{8,0},{9,1},{10,... | collective-permute-start | bytes 344072 | tf_op jit(solution)/shard_map/ppermute | solution.py:380
  15.6 4.3 %collective-permute-start.7 = (f32[16,512]{1,0:T(8,128)S(1)}, f32[16,512]{1,0:T(8,128)S(1)}, u32[]{:S(2)}, u32[]{:S(2)}) collective-permute-start(f32[16,512]{1,0:T(8,128)S(1)} %dynamic-slice_select_fusion.refs_4_), channel_id=1, source_target_pairs={{0,1},{1,0},{2,3},{3,2},{4,5},{5,4},{6,7},{7,6},{8,9},{9,8},{10,11... | collective-permute-start | bytes 98312 | tf_op jit(solution)/shard_map/ppermute | solution.py:380
  16.8 3.2 %collective-permute-start.3 = (bf16[4,448,128]{2,1,0:T(8,128)(2,1)S(1)}, bf16[4,448,128]{2,1,0:T(8,128)(2,1)S(1)}, u32[]{:S(2)}, u32[]{:S(2)}) collective-permute-start(bf16[4,448,128]{2,1,0:T(8,128)(2,1)S(1)} %batch.2.refs_0_), channel_id=1, source_target_pairs={{0,2},{1,3},{2,0},{3,1},{4,6},{5,7},{6,4},{7,5},{8,10},{9,11},{10,... | collective-permute-start | bytes 1376264 | tf_op jit(solution)/shard_map/ppermute | solution.py:380
  20.0 1.9 %collective-permute-start.9 = (bf16[4,448,128]{2,1,0:T(8,128)(2,1)S(1)}, bf16[4,448,128]{2,1,0:T(8,128)(2,1)S(1)}, u32[]{:S(2)}, u32[]{:S(2)}) collective-permute-start(bf16[4,448,128]{2,1,0:T(8,128)(2,1)S(1)} %batch.3.refs_2_), channel_id=1, source_target_pairs={{0,2},{1,3},{2,0},{3,1},{4,6},{5,7},{6,4},{7,5},{8,10},{9,11},{10,... | collective-permute-start | bytes 1376264 | tf_op jit(solution)/shard_map/ppermute | solution.py:380
  30.7 5.2 %collective-permute-start.10 = (bf16[16,1024]{1,0:T(8,128)(2,1)S(1)}, bf16[16,1024]{1,0:T(8,128)(2,1)S(1)}, u32[]{:S(2)}, u32[]{:S(2)}) collective-permute-start(bf16[16,1024]{1,0:T(8,128)(2,1)S(1)} %get-tuple-element.22), channel_id=1, source_target_pairs={{0,16},{16,0},{1,17},{17,1},{2,18},{18,2},{3,19},{19,3},{4,20},{20... | collective-permute-start | bytes 98312 | tf_op jit(solution)/shard_map/ppermute | solution.py:403
  44.1 1.3 %collective-permute-start.11 = (f32[2,16,512]{2,1,0:T(8,128)S(1)}, f32[2,16,512]{2,1,0:T(8,128)S(1)}, u32[]{:S(2)}, u32[]{:S(2)}) collective-permute-start(f32[2,16,512]{2,1,0:T(8,128)S(1)} %cascade_1.1.mine), channel_id=1, source_target_pairs={{0,2},{1,3},{2,0},{3,1},{4,6},{5,7},{6,4},{7,5},{8,10},{9,11},{10,... | collective-permute-start | bytes 196616 | tf_op jit(solution)/shard_map/ppermute | solution.py:380

commit v2 on v0

--- a/solution.py
+++ b/solution.py
@@ -13,6 +13,7 @@
 BLOCKS_PER_LANES = LANES // BLOCK
 PACKED = LANES - BLOCK
 DEGREE = 4
+GROUP_ROWS = 32
 SMALL_GRANT = 4 * 1024 * 1024
 CORES = 2
 
@@ -141,37 +142,41 @@
 def fill_masks(masks):
     row = lax.broadcasted_iota(jnp.int32, (LANES, LANES), 0)
     lane = lax.broadcasted_iota(jnp.int32, (LANES, LANES), 1)
-    masks[0] = (lane >= row // BLOCK * BLOCK).astype(jnp.float32).astype(jnp.bfloat16)
-    masks[1] = (row >= lane // BLOCK * BLOCK).astype(jnp.float32).astype(jnp.bfloat16)
-    masks[2] = (row < LANES - 1).astype(jnp.float32).astype(jnp.bfloat16)
+    masks[0] = (row < LANES - 1).astype(jnp.float32).astype(jnp.bfloat16)
     own = lane // BLOCK != (row // BLOCK + BLOCKS_PER_LANES - 1) % BLOCKS_PER_LANES
-    masks[3] = own.astype(jnp.float32).astype(jnp.bfloat16)
-
-
-def expand(folds, slot, masks, upper, lower):
-    tiles = upper.shape[0]
+    masks[1] = own.astype(jnp.float32).astype(jnp.bfloat16)
+    masks[2] = (row >= lane // BLOCK * BLOCK).astype(jnp.float32).astype(jnp.bfloat16)
+
+
+def expand(folds, slot, masks, both):
+    tiles = both.shape[0] // LANES
     lane = lax.broadcasted_iota(jnp.int32, (1, LANES), 1)
     eighth = folds[slot, (tiles - 1) * PACKED : (tiles - 1) * PACKED + BLOCK, :]
     last_row = eighth.astype(jnp.float32)[BLOCK - 1 :, :]
     last_row = jnp.where(lane >= PACKED, last_row, -float(LANES))
     first = jnp.max(last_row).astype(jnp.int32)
+    near, far = [], []
     for t in range(tiles):
         packed = folds[slot, t * PACKED : (t + 1) * PACKED, :]
-        own = packed * masks[3, :PACKED, :]
+        own = packed * masks[1, :PACKED, :]
         rest = packed - own
         eighth = [rest[b : b + BLOCK] for b in range(0, PACKED, BLOCK)]
         while len(eighth) > 1:
             eighth = [sum(eighth[i : i + 2][1:], eighth[i]) for i in range(0, len(eighth), 2)]
         run = jnp.concatenate([own, eighth[0]], axis=0)
         if t == tiles - 1:
-            run = run * masks[2]
-        near = run * masks[0]
-        upper[t, :, :LANES] = near
-        upper[t, :, LANES:] = run - near
+            run = run * masks[0]
+        both[t * LANES : (t + 1) * LANES, :LANES] = run
         turned = run.T
-        near = turned * masks[1]
-        lower[t, :, :LANES] = near
-        lower[(t + 1) % tiles, :, LANES:] = turned - near
+        near.append(turned * masks[2])
+        far.append(turned - near[-1])
+    for t in range(tiles):
+        turned = (near[t] + far[t - 1]).astype(jnp.float32)
+        turned = pltpu.roll(turned, first * BLOCK & (LANES - 1), 1).astype(jnp.bfloat16)
+        for b in range(BLOCKS_PER_LANES):
+            at = (t * BLOCKS_PER_LANES + b + first) & (tiles * BLOCKS_PER_LANES - 1)
+            here = pl.ds(pl.multiple_of(at * BLOCK, BLOCK), BLOCK)
+            both[here, LANES:] = turned[b * BLOCK : (b + 1) * BLOCK]
     return first
 
 
@@ -185,43 +190,57 @@
     return parts
 
 
-def banded_product(v, upper, lower, start):
-    tiles = len(v)
+def banded_product(v, both, start):
+    tiles, fields = len(v), v[0].shape[0]
     whole = start >> 3
     fine = (start & (BLOCKS_PER_LANES - 1)) * BLOCK
     lane = lax.broadcasted_iota(jnp.int32, v[0].shape, 1)
-    turned = [pltpu.roll(part, (LANES - fine) & (LANES - 1), 1) for part in v]
-    moved = turn(
+    groups = LANES // GROUP_ROWS
+    keeps = [
+        (lane >= c * GROUP_ROWS).astype(jnp.float32).astype(jnp.bfloat16)
+        for c in range(1, groups)
+    ]
+    upper, lower = [[None] * tiles for _ in range(2)], [[None] * tiles for _ in range(2)]
+    for t in range(tiles):
+        part = v[t].astype(jnp.bfloat16)
+        spread = jnp.concatenate([part] + [part * keep for keep in keeps], axis=0)
+        product = jnp.dot(
+            spread,
+            both[t * LANES : (t + 1) * LANES, :],
+            preferred_element_type=jnp.float32,
+        )
+        sums = [product[c * fields : (c + 1) * fields] for c in range(groups)]
+        following = jnp.zeros_like(v[t])
+        same = sums[-1][:, LANES:]
+        for c in range(groups - 2, -1, -1):
+            here = lane < (c + 1) * GROUP_ROWS
+            following = jnp.where(here, sums[c + 1][:, :LANES], following)
+            same = jnp.where(here, sums[c][:, LANES:], same)
+        upper[0][t], upper[1][t] = sums[0][:, :LANES] - following, following
+        lower[0][t], lower[1][t] = same, sums[0][:, LANES:] - same
+    turned = [pltpu.roll(upper[0][t] + upper[1][t - 1], fine, 1) for t in range(tiles)]
+    ahead = turn(
+        [jnp.where(lane >= fine, turned[t], turned[t - 1]) for t in range(tiles)], -whole
+    )
+    back = (LANES - fine) & (LANES - 1)
+    turned = [
+        pltpu.roll(lower[0][t] + lower[1][(t + 1) % tiles], back, 1) for t in range(tiles)
+    ]
+    behind = turn(
         [
-            jnp.where(lane < LANES - fine, turned[u], turned[(u + 1) % tiles])
-            for u in range(tiles)
+            jnp.where(lane < LANES - fine, turned[t], turned[(t + 1) % tiles])
+            for t in range(tiles)
         ],
         whole,
     )
-    first = [
-        jnp.dot(v[t].astype(jnp.bfloat16), upper[t], preferred_element_type=jnp.float32)
-        for t in range(tiles)
-    ]
-    second = [
-        jnp.dot(moved[u].astype(jnp.bfloat16), lower[u], preferred_element_type=jnp.float32)
-        for u in range(tiles)
-    ]
-    sums = [first[t][:, :LANES] + first[t - 1][:, LANES:] for t in range(tiles)]
-    turned = [pltpu.roll(part, fine, 1) for part in sums]
-    ahead = turn(
-        [jnp.where(lane >= fine, turned[u], turned[u - 1]) for u in range(tiles)], -whole
-    )
-    return [
-        ahead[u] - (second[u][:, :LANES] + second[(u + 1) % tiles][:, LANES:])
-        for u in range(tiles)
-    ]
-
-
-def run_layer(x, sign, upper, lower, start):
+    return [a - b for a, b in zip(ahead, behind)]
+
+
+def run_layer(x, sign, both, start):
     v = x
     for divisor in range(DEGREE, 0, -1):
         scale = sign * (1.0 / divisor)
-        product = banded_product(v, upper, lower, start)
+        product = banded_product(v, both, start)
         v = [part + scale * term for part, term in zip(x, product)]
     return v
 
@@ -232,7 +251,7 @@
         pieces += [(refs[0], index) for index in range(count)]
         refs = refs[1:]
     others, refs = refs[: len(row_masks)], refs[len(row_masks) :]
-    own, kept, upper, lower, starts, send, folds, masks, field = refs
+    own, kept, both, starts, send, folds, masks, field = refs
     place(pieces, distances[1], folds)
     fill_masks(masks)
     place_field(own, list(zip(others, row_masks)), field)
@@ -242,14 +261,14 @@
 
     def prepare(k):
         slot = jnp.where(forward, k, GROUP - 1 - k)
-        start = expand(folds, slot, masks, upper.at[k], lower.at[k])
+        start = expand(folds, slot, masks, both.at[k])
         starts[k : k + 1, :] = jnp.full((1, LANES), start, jnp.int32)
         return start
 
     start = prepare(0)
     for k in range(GROUP):
         following = prepare(k + 1) if k + 1 < GROUP else None
-        x = run_layer(x, sign, upper.at[k], lower.at[k], start)
+        x = run_layer(x, sign, both.at[k], start)
         start = following
     mine = own_panel(x, kept.shape[-1])
     kept[0] = mine
@@ -258,7 +277,7 @@
 
 
 def cascade_next_kernel(step, groups, *refs):
-    upper, lower, starts, field, before, kept, *send = refs
+    both, starts, field, before, kept, *send = refs
     panel = kept.shape[-1]
     group = lax.axis_index("layer") // GROUP
     forward = group == step
@@ -271,7 +290,7 @@
     order = [jnp.where(same_order, k, GROUP - 1 - k) for k in range(GROUP)]
     begin = [jnp.max(starts[pl.ds(at, 1), :]) for at in order]
     for at, start in zip(order, begin):
-        x = run_layer(x, sign, upper.at[at], lower.at[at], start)
+        x = run_layer(x, sign, both.at[at], start)
     mine = own_panel(x, panel)
     kept[0] = jnp.where(forward, mine, before[0])
     kept[1] = jnp.where(backward, mine, before[1])
@@ -319,21 +338,19 @@
     count, panel = field.shape
     tiles = orders // LANES
     vmem = pl.BlockSpec(memory_space=pltpu.VMEM)
-    window = jax.ShapeDtypeStruct((GROUP, tiles, LANES, 2 * LANES), jnp.bfloat16)
     return pl.pallas_call(
         functools.partial(cascade_first_kernel, distances, row_masks),
         out_shape=[
             jax.ShapeDtypeStruct((2, count, panel), jnp.float32),
-            window,
-            window,
+            jax.ShapeDtypeStruct((GROUP, orders, 2 * LANES), jnp.bfloat16),
             jax.ShapeDtypeStruct((GROUP, LANES), jnp.int32),
             jax.ShapeDtypeStruct((count, orders), jnp.bfloat16),
         ],
         in_specs=[vmem] * (len(batches) + len(others) + 1),
-        out_specs=[vmem] * 5,
+        out_specs=[vmem] * 4,
         scratch_shapes=[
             pltpu.VMEM((GROUP, tiles * PACKED, LANES), jnp.bfloat16),
-            pltpu.VMEM((4, LANES, LANES), jnp.bfloat16),
+            pltpu.VMEM((3, LANES, LANES), jnp.bfloat16),
             pltpu.VMEM((tiles, count, LANES), jnp.float32),
         ],
         compiler_params=pltpu.CompilerParams(vmem_limit_bytes=24 * 1024 * 1024),
@@ -341,7 +358,7 @@
     )(*batches, *others, field)
 
 
-def run_next(step, groups, upper, lower, starts, field, kept):
+def run_next(step, groups, both, starts, field, kept):
     vmem = pl.BlockSpec(memory_space=pltpu.VMEM)
     out_shape = [jax.ShapeDtypeStruct(kept.shape, jnp.float32)]
     if step < groups - 1:
@@ -349,11 +366,11 @@
     return pl.pallas_call(
         functools.partial(cascade_next_kernel, step, groups),
         out_shape=out_shape,
-        in_specs=[vmem] * 5,
+        in_specs=[vmem] * 4,
         out_specs=[vmem] * len(out_shape),
         compiler_params=pltpu.CompilerParams(vmem_limit_bytes=24 * 1024 * 1024),
         name=f"cascade_{step}",
-    )(upper, lower, starts, field, kept)
+    )(both, starts, field, kept)
 
 
 def gather_batches(own, corner, across, rows):
@@ -417,7 +434,7 @@
     for mask in range(1, rows - 1):
         others.append(across(whole, ((0, mask), (0, mask))))
         row_masks.append(mask)
-    kept, upper, lower, starts, send = run_first(
+    kept, both, starts, send = run_first(
         batches, distances, others, tuple(row_masks), field, orders
     )
     for step in range(1, groups):
@@ -428,7 +445,7 @@
             pairs.append((forward_from, forward_from + GROUP * rows))
             pairs.append((adjoint_from, adjoint_from - GROUP * rows))
         field = lax.ppermute(send, ("layer", "row"), pairs)
-        kept, *send = run_next(step, groups, upper, lower, starts, field, kept)
+        kept, *send = run_next(step, groups, both, starts, field, kept)
         send = send[0] if send else None
     return tuple(join(kept, across(kept, ((1, 0), (1, 0)))))
 

time: 45.3 us -> 48.1 us (1.062)
  Pallas kernels: 18.1 us -> 20.9 us
    pallas_call x1, Pallas kernels: 8.85 us -> 10.3 us  [run_first(): pl.pallas_call(functools.partial(cascade_first_kernel, distances, row_mas...]
    pallas_call x1, Pallas kernels: 8.19 us -> 9.57 us  [run_next(): pl.pallas_call(functools.partial(cascade_next_kernel, step, groups), out_...]
where the time goes in v2:
time: 48.1 us; the launch traced here: 47.9 us
  Pallas kernels  20.9 us (43%)
  starting transfers between devices  13.5 us (28%)
  waiting for transfers between devices  9.45 us (20%)
  between operations  2.01 us (4%)
  local copies, waits for them, and re-layouts  1.22 us (3%)
  other arithmetic  0.78 us (2%)
    ppermute x10, starting transfers between devices, across(): return lax.ppermute(array, ('layer', 'row'), pairs)  10.8 us
    pallas_call x1, Pallas kernels, run_first(): pl.pallas_call(functools.partial(cascade_first_kernel, distances, row_mas...  10.3 us
    pallas_call x1, Pallas kernels, run_next(): pl.pallas_call(functools.partial(cascade_next_kernel, step, groups), out_...  9.57 us
    ppermute x10, waiting for transfers between devices, across(): return lax.ppermute(array, ('layer', 'row'), pairs)  7.14 us
    ppermute x1, starting transfers between devices, on_device(): field = lax.ppermute(send, ('layer', 'row'), pairs)  2.66 us
    ppermute x1, waiting for transfers between devices, on_device(): field = lax.ppermute(send, ('layer', 'row'), pairs)  2.31 us
    unnamed x2, local copies, waits for them, and re-layouts  1.22 us
  transfers between devices with their start and end apart: 11, of which 7 were waited for; matrix products, arithmetic and copies ran while one was open for 2% of the time, Pallas kernels for 0%

profile of v2, /device:TPU:0, one launch (start us, length us, event | category | flops | bytes accessed | tf_op | source)
XLA Modules:
  0.0 47.9 jit_solution(14143229488630483668)
XLA Ops:
  1.9 1.2 %copy-done = bf16[1,512,1024]{2,1,0:T(8,128)(2,1)S(1)} copy-done((bf16[1,512,1024]{2,1,0:T(8,128)(2,1)S(1)}, bf16[1,512,1024]{2,1,0:T(8,128)(2,1)}, u32[]{:S(2)}) %copy-start) | copy-done | bytes 1048600
  3.1 0.3 fold.1.refs_0_.folded
  3.5 3.1 %collective-permute-start.2 = (bf16[448,128]{1,0:T(8,128)(2,1)S(1)}, bf16[448,128]{1,0:T(8,128)(2,1)S(1)}, u32[]{:S(2)}, u32[]{:S(2)}) collective-permute-start(bf16[448,128]{1,0:T(8,128)(2,1)S(1)} %fold.1.refs_0_.folded), channel_id=1, source_target_pairs={{0,8},{1,9},{2,3},{3,2},{4,12},{5,13},{6,7},{7,6},{8,0},{9,1},{10,... | collective-permute-start | bytes 344072 | tf_op jit(solution)/shard_map/ppermute | solution.py:423
  6.6 1.5 %collective-permute-start.1 = (bf16[448,128]{1,0:T(8,128)(2,1)S(1)}, bf16[448,128]{1,0:T(8,128)(2,1)S(1)}, u32[]{:S(2)}, u32[]{:S(2)}) collective-permute-start(bf16[448,128]{1,0:T(8,128)(2,1)S(1)} %fold.1.refs_0_.folded), channel_id=1, source_target_pairs={{0,4},{1,5},{2,10},{3,11},{4,0},{5,1},{6,14},{7,15},{8,12},{9,13},... | collective-permute-start | bytes 344072 | tf_op jit(solution)/shard_map/ppermute | solution.py:423
  8.1 1.5 %collective-permute-start = (bf16[448,128]{1,0:T(8,128)(2,1)S(1)}, bf16[448,128]{1,0:T(8,128)(2,1)S(1)}, u32[]{:S(2)}, u32[]{:S(2)}) collective-permute-start(bf16[448,128]{1,0:T(8,128)(2,1)S(1)} %fold.1.refs_0_.folded), channel_id=1, source_target_pairs={{0,1},{1,0},{2,6},{3,7},{4,5},{5,4},{6,2},{7,3},{8,9},{9,8},{10,14... | collective-permute-start | bytes 344072 | tf_op jit(solution)/shard_map/ppermute | solution.py:423
  9.6 0.8 %dynamic-slice_select_fusion.field.refs_5_ = f32[16,512]{1,0:T(8,128)S(1)} fusion(f32[32,512]{1,0:T(8,128)} %param.9, s32[]{:T(128)S(6)} %select_n.26, f32[32,512]{1,0:T(8,128)} %param.8, pred[]{:T(512)S(6)} %eq.5), kind=kLoop, calls=%fused_computation | loop fusion | flops 8192 | bytes 98309 | tf_op jit(solution)/shard_map/jit(_where)/select_n | solution.py:429
  10.4 0.1 collective-permute-start.7
  10.5 1.9 %collective-permute-start.6 = (bf16[448,128]{1,0:T(8,128)(2,1)S(1)}, bf16[448,128]{1,0:T(8,128)(2,1)S(1)}, u32[]{:S(2)}, u32[]{:S(2)}) collective-permute-start(bf16[448,128]{1,0:T(8,128)(2,1)S(1)} %collective-permute-done.2.refs_3_), channel_id=1, source_target_pairs={{0,4},{1,5},{2,10},{3,11},{4,0},{5,1},{6,14},{7,15},{8,12},{9,13},... | collective-permute-start | bytes 344072 | tf_op jit(solution)/shard_map/ppermute | solution.py:423
  12.4 0.5 collective-permute-done.1.refs_2_
  12.9 1.0 %collective-permute-start.4 = (bf16[448,128]{1,0:T(8,128)(2,1)S(1)}, bf16[448,128]{1,0:T(8,128)(2,1)S(1)}, u32[]{:S(2)}, u32[]{:S(2)}) collective-permute-start(bf16[448,128]{1,0:T(8,128)(2,1)S(1)} %collective-permute-done.1.refs_2_), channel_id=1, source_target_pairs={{0,1},{1,0},{2,6},{3,7},{4,5},{5,4},{6,2},{7,3},{8,9},{9,8},{10,14... | collective-permute-start | bytes 344072 | tf_op jit(solution)/shard_map/ppermute | solution.py:423
  13.8 1.6 %collective-permute-start.5 = (bf16[448,128]{1,0:T(8,128)(2,1)S(1)}, bf16[448,128]{1,0:T(8,128)(2,1)S(1)}, u32[]{:S(2)}, u32[]{:S(2)}) collective-permute-start(bf16[448,128]{1,0:T(8,128)(2,1)S(1)} %collective-permute-done.refs_1_), channel_id=1, source_target_pairs={{0,8},{1,9},{2,3},{3,2},{4,12},{5,13},{6,7},{7,6},{8,0},{9,1},{10,... | collective-permute-start | bytes 344072 | tf_op jit(solution)/shard_map/ppermute | solution.py:423
  15.4 0.1 collective-permute-start.3
  15.5 2.5 %collective-permute-done.7.refs_3_.refs_4_ = bf16[512,128]{1,0:T(8,128)(2,1)S(1)} collective-permute-done((bf16[512,128]{1,0:T(8,128)(2,1)S(1)}, bf16[512,128]{1,0:T(8,128)(2,1)S(1)}, u32[]{:S(2)}, u32[]{:S(2)}) %collective-permute-start.7) | collective-permute-done | bytes 131104 | tf_op jit(solution)/shard_map/ppermute | solution.py:423
  18.0 0.1 collective-permute-done.6.refs_2_
  18.1 1.0 %collective-permute-done.4.refs_0_ = bf16[448,128]{1,0:T(8,128)(2,1)S(1)} collective-permute-done((bf16[448,128]{1,0:T(8,128)(2,1)S(1)}, bf16[448,128]{1,0:T(8,128)(2,1)S(1)}, u32[]{:S(2)}, u32[]{:S(2)}) %collective-permute-start.4) | collective-permute-done | bytes 114720 | tf_op jit(solution)/shard_map/ppermute | solution.py:423
  19.2 0.1 collective-permute-start.8
  19.3 1.8 %collective-permute-done.8.refs_3_ = bf16[4,448,128]{2,1,0:T(8,128)(2,1)S(1)} collective-permute-done((bf16[4,448,128]{2,1,0:T(8,128)(2,1)S(1)}, bf16[4,448,128]{2,1,0:T(8,128)(2,1)S(1)}, u32[]{:S(2)}, u32[]{:S(2)}) %collective-permute-start.8) | collective-permute-done | bytes 458784 | tf_op jit(solution)/shard_map/ppermute | solution.py:423
  21.1 10.3 %cascade_first.1 = (f32[2,16,512]{2,1,0:T(8,128)S(1)}, bf16[8,1024,256]{2,1,0:T(8,128)(2,1)S(1)}, s32[8,128]{1,0:T(8,128)S(1)}, bf16[16,1024]{1,0:T(8,128)(2,1)S(1)}) custom-call(bf16[4,448,128]{2,1,0:T(8,128)(2,1)S(1)} %batch.2.refs_0_, bf16[4,448,128]{2,1,0:T(8,128)(2,1)S(1)} %collective-permute-done.3.refs_1_, bf16[4,448,128]{2,1,0:T(8,128)(2,1)S(1)} %batch.3.refs_2_, ...), custom_call_target="tpu_custom_call" | custom-call | tf_op jit(solution)/shard_map/cascade_first/pallas_call | solution.py:341
  31.3 2.7 %collective-permute-start.9 = (bf16[16,1024]{1,0:T(8,128)(2,1)S(1)}, bf16[16,1024]{1,0:T(8,128)(2,1)S(1)}, u32[]{:S(2)}, u32[]{:S(2)}) collective-permute-start(bf16[16,1024]{1,0:T(8,128)(2,1)S(1)} %get-tuple-element.14), channel_id=1, source_target_pairs={{0,16},{16,0},{1,17},{17,1},{2,18},{18,2},{3,19},{19,3},{4,20},{20... | collective-permute-start | bytes 98312 | tf_op jit(solution)/shard_map/ppermute | solution.py:447
  34.0 2.3 %collective-permute-done.9.refs_2_ = bf16[16,1024]{1,0:T(8,128)(2,1)S(1)} collective-permute-done((bf16[16,1024]{1,0:T(8,128)(2,1)S(1)}, bf16[16,1024]{1,0:T(8,128)(2,1)S(1)}, u32[]{:S(2)}, u32[]{:S(2)}) %collective-permute-start.9) | collective-permute-done | bytes 32800 | tf_op jit(solution)/shard_map/ppermute | solution.py:447
  36.3 9.6 %cascade_1.1.mine = f32[2,16,512]{2,1,0:T(8,128)S(1)} custom-call(bf16[8,1024,256]{2,1,0:T(8,128)(2,1)S(1)} %get-tuple-element.12.refs_0_, s32[8,128]{1,0:T(8,128)S(1)} %get-tuple-element.13.refs_1_, bf16[16,1024]{1,0:T(8,128)(2,1)S(1)} %collective-permute-done.9.refs_2_, f32[2,16,512]{2,1,0:T(8,128)S(1)} %get-tuple-element.15.refs_3_), custom_call_target="tpu_custom_call" | custom-call | tf_op jit(solution)/shard_map/cascade_1/pallas_call | solution.py:366
  45.9 0.1 collective-permute-start.10
  46.0 1.2 %collective-permute-done.10.theirs = f32[2,16,512]{2,1,0:T(8,128)S(1)} collective-permute-done((f32[2,16,512]{2,1,0:T(8,128)S(1)}, f32[2,16,512]{2,1,0:T(8,128)S(1)}, u32[]{:S(2)}, u32[]{:S(2)}) %collective-permute-start.10) | collective-permute-done | bytes 65568 | tf_op jit(solution)/shard_map/ppermute | solution.py:423
  47.2 0.7 %join.1 = (f32[1,32,512]{2,1,0:T(8,128)}, f32[1,32,512]{2,1,0:T(8,128)}) custom-call(f32[2,16,512]{2,1,0:T(8,128)S(1)} %cascade_1.1.mine, f32[2,16,512]{2,1,0:T(8,128)S(1)} %collective-permute-done.10.theirs), custom_call_target="tpu_custom_call" | custom-call | tf_op jit(solution)/shard_map/join/pallas_call | solution.py:327
  (8 shorter events, 0.1 us)
Async XLA Ops:
  1.9 1.2 %copy-start = (bf16[1,512,1024]{2,1,0:T(8,128)(2,1)S(1)}, bf16[1,512,1024]{2,1,0:T(8,128)(2,1)}, u32[]{:S(2)}) copy-start(bf16[1,512,1024]{2,1,0:T(8,128)(2,1)} %coupling_ref.1) | copy-start | bytes 3145732
  3.5 7.0 %collective-permute-start.2 = (bf16[448,128]{1,0:T(8,128)(2,1)S(1)}, bf16[448,128]{1,0:T(8,128)(2,1)S(1)}, u32[]{:S(2)}, u32[]{:S(2)}) collective-permute-start(bf16[448,128]{1,0:T(8,128)(2,1)S(1)} %fold.1.refs_0_.folded), channel_id=1, source_target_pairs={{0,8},{1,9},{2,3},{3,2},{4,12},{5,13},{6,7},{7,6},{8,0},{9,1},{10,... | collective-permute-start | bytes 344072 | tf_op jit(solution)/shard_map/ppermute | solution.py:423
  6.6 6.3 %collective-permute-start.1 = (bf16[448,128]{1,0:T(8,128)(2,1)S(1)}, bf16[448,128]{1,0:T(8,128)(2,1)S(1)}, u32[]{:S(2)}, u32[]{:S(2)}) collective-permute-start(bf16[448,128]{1,0:T(8,128)(2,1)S(1)} %fold.1.refs_0_.folded), channel_id=1, source_target_pairs={{0,4},{1,5},{2,10},{3,11},{4,0},{5,1},{6,14},{7,15},{8,12},{9,13},... | collective-permute-start | bytes 344072 | tf_op jit(solution)/shard_map/ppermute | solution.py:423
  8.1 5.8 %collective-permute-start = (bf16[448,128]{1,0:T(8,128)(2,1)S(1)}, bf16[448,128]{1,0:T(8,128)(2,1)S(1)}, u32[]{:S(2)}, u32[]{:S(2)}) collective-permute-start(bf16[448,128]{1,0:T(8,128)(2,1)S(1)} %fold.1.refs_0_.folded), channel_id=1, source_target_pairs={{0,1},{1,0},{2,6},{3,7},{4,5},{5,4},{6,2},{7,3},{8,9},{9,8},{10,14... | collective-permute-start | bytes 344072 | tf_op jit(solution)/shard_map/ppermute | solution.py:423
  10.4 7.6 %collective-permute-start.7 = (bf16[512,128]{1,0:T(8,128)(2,1)S(1)}, bf16[512,128]{1,0:T(8,128)(2,1)S(1)}, u32[]{:S(2)}, u32[]{:S(2)}) collective-permute-start(bf16[512,128]{1,0:T(8,128)(2,1)S(1)} %corner.1), channel_id=1, source_target_pairs={{0,13},{1,12},{2,15},{3,14},{4,9},{5,8},{6,11},{7,10},{8,5},{9,4},... | collective-permute-start | bytes 393224 | tf_op jit(solution)/shard_map/ppermute | solution.py:423
  10.5 7.7 %collective-permute-start.6 = (bf16[448,128]{1,0:T(8,128)(2,1)S(1)}, bf16[448,128]{1,0:T(8,128)(2,1)S(1)}, u32[]{:S(2)}, u32[]{:S(2)}) collective-permute-start(bf16[448,128]{1,0:T(8,128)(2,1)S(1)} %collective-permute-done.2.refs_3_), channel_id=1, source_target_pairs={{0,4},{1,5},{2,10},{3,11},{4,0},{5,1},{6,14},{7,15},{8,12},{9,13},... | collective-permute-start | bytes 344072 | tf_op jit(solution)/shard_map/ppermute | solution.py:423
  12.9 6.3 %collective-permute-start.4 = (bf16[448,128]{1,0:T(8,128)(2,1)S(1)}, bf16[448,128]{1,0:T(8,128)(2,1)S(1)}, u32[]{:S(2)}, u32[]{:S(2)}) collective-permute-start(bf16[448,128]{1,0:T(8,128)(2,1)S(1)} %collective-permute-done.1.refs_2_), channel_id=1, source_target_pairs={{0,1},{1,0},{2,6},{3,7},{4,5},{5,4},{6,2},{7,3},{8,9},{9,8},{10,14... | collective-permute-start | bytes 344072 | tf_op jit(solution)/shard_map/ppermute | solution.py:423
  13.8 5.3 %collective-permute-start.5 = (bf16[448,128]{1,0:T(8,128)(2,1)S(1)}, bf16[448,128]{1,0:T(8,128)(2,1)S(1)}, u32[]{:S(2)}, u32[]{:S(2)}) collective-permute-start(bf16[448,128]{1,0:T(8,128)(2,1)S(1)} %collective-permute-done.refs_1_), channel_id=1, source_target_pairs={{0,8},{1,9},{2,3},{3,2},{4,12},{5,13},{6,7},{7,6},{8,0},{9,1},{10,... | collective-permute-start | bytes 344072 | tf_op jit(solution)/shard_map/ppermute | solution.py:423
  15.4 3.8 %collective-permute-start.3 = (bf16[4,448,128]{2,1,0:T(8,128)(2,1)S(1)}, bf16[4,448,128]{2,1,0:T(8,128)(2,1)S(1)}, u32[]{:S(2)}, u32[]{:S(2)}) collective-permute-start(bf16[4,448,128]{2,1,0:T(8,128)(2,1)S(1)} %batch.2.refs_0_), channel_id=1, source_target_pairs={{0,2},{1,3},{2,0},{3,1},{4,6},{5,7},{6,4},{7,5},{8,10},{9,11},{10,... | collective-permute-start | bytes 1376264 | tf_op jit(solution)/shard_map/ppermute | solution.py:423
  19.2 1.9 %collective-permute-start.8 = (bf16[4,448,128]{2,1,0:T(8,128)(2,1)S(1)}, bf16[4,448,128]{2,1,0:T(8,128)(2,1)S(1)}, u32[]{:S(2)}, u32[]{:S(2)}) collective-permute-start(bf16[4,448,128]{2,1,0:T(8,128)(2,1)S(1)} %batch.3.refs_2_), channel_id=1, source_target_pairs={{0,2},{1,3},{2,0},{3,1},{4,6},{5,7},{6,4},{7,5},{8,10},{9,11},{10,... | collective-permute-start | bytes 1376264 | tf_op jit(solution)/shard_map/ppermute | solution.py:423
  31.3 5.0 %collective-permute-start.9 = (bf16[16,1024]{1,0:T(8,128)(2,1)S(1)}, bf16[16,1024]{1,0:T(8,128)(2,1)S(1)}, u32[]{:S(2)}, u32[]{:S(2)}) collective-permute-start(bf16[16,1024]{1,0:T(8,128)(2,1)S(1)} %get-tuple-element.14), channel_id=1, source_target_pairs={{0,16},{16,0},{1,17},{17,1},{2,18},{18,2},{3,19},{19,3},{4,20},{20... | collective-permute-start | bytes 98312 | tf_op jit(solution)/shard_map/ppermute | solution.py:447
  45.9 1.3 %collective-permute-start.10 = (f32[2,16,512]{2,1,0:T(8,128)S(1)}, f32[2,16,512]{2,1,0:T(8,128)S(1)}, u32[]{:S(2)}, u32[]{:S(2)}) collective-permute-start(f32[2,16,512]{2,1,0:T(8,128)S(1)} %cascade_1.1.mine), channel_id=1, source_target_pairs={{0,2},{1,3},{2,0},{3,1},{4,6},{5,7},{6,4},{7,5},{8,10},{9,11},{10,... | collective-permute-start | bytes 196616 | tf_op jit(solution)/shard_map/ppermute | solution.py:423

commit v3 on v0

--- a/solution.py
+++ b/solution.py
@@ -232,7 +232,7 @@
         pieces += [(refs[0], index) for index in range(count)]
         refs = refs[1:]
     others, refs = refs[: len(row_masks)], refs[len(row_masks) :]
-    own, kept, upper, lower, starts, send, folds, masks, field = refs
+    own, mine, upper, lower, starts, send, folds, masks, field = refs
     place(pieces, distances[1], folds)
     fill_masks(masks)
     place_field(own, list(zip(others, row_masks)), field)
@@ -251,18 +251,14 @@
         following = prepare(k + 1) if k + 1 < GROUP else None
         x = run_layer(x, sign, upper.at[k], lower.at[k], start)
         start = following
-    mine = own_panel(x, kept.shape[-1])
-    kept[0] = mine
-    kept[1] = mine
+    mine[...] = own_panel(x, mine.shape[-1])
     write_whole(x, send)
 
 
 def cascade_next_kernel(step, groups, *refs):
-    upper, lower, starts, field, before, kept, *send = refs
-    panel = kept.shape[-1]
+    upper, lower, starts, field, mine, *send = refs
     group = lax.axis_index("layer") // GROUP
     forward = group == step
-    backward = group == groups - 1 - step
     sign = jnp.where(forward, -1.0, 1.0)
     same_order = forward == (group == 0)
     x = field[...].astype(jnp.float32)
@@ -272,9 +268,7 @@
     begin = [jnp.max(starts[pl.ds(at, 1), :]) for at in order]
     for at, start in zip(order, begin):
         x = run_layer(x, sign, upper.at[at], lower.at[at], start)
-    mine = own_panel(x, panel)
-    kept[0] = jnp.where(forward, mine, before[0])
-    kept[1] = jnp.where(backward, mine, before[1])
+    mine[...] = own_panel(x, mine.shape[-1])
     if send:
         write_whole(x, *send)
 
@@ -294,25 +288,29 @@
     return jnp.concatenate(mine, axis=1)
 
 
-def join_kernel(mine, theirs, *outs):
+def join_kernel(groups, *refs):
     core = lax.axis_index("layer") % CORES
-    count = mine.shape[1]
-    for kind, out in enumerate(outs):
-        for part, at in ((mine, core), (theirs, 1 - core)):
-            out[0, pl.ds(pl.multiple_of(at * count, count), count), :] = part[kind]
+    group = lax.axis_index("layer") // GROUP
+    count = refs[0].shape[0]
+    for out, step in zip(refs[-2:], (group, groups - 1 - group)):
+        for parts, at in ((refs[:groups], core), (refs[groups : 2 * groups], 1 - core)):
+            chosen = parts[0][...]
+            for index in range(1, groups):
+                chosen = jnp.where(step == index, parts[index][...], chosen)
+            out[0, pl.ds(pl.multiple_of(at * count, count), count), :] = chosen
 
 
 def join(mine, theirs):
-    kinds, count, panel = mine.shape
-    vmem = pl.BlockSpec(memory_space=pltpu.VMEM)
-    return pl.pallas_call(
-        join_kernel,
-        out_shape=[jax.ShapeDtypeStruct((1, CORES * count, panel), mine.dtype)] * kinds,
-        in_specs=[vmem] * 2,
-        out_specs=[vmem] * kinds,
+    count, panel = mine[0].shape
+    vmem = pl.BlockSpec(memory_space=pltpu.VMEM)
+    return pl.pallas_call(
+        functools.partial(join_kernel, len(mine)),
+        out_shape=[jax.ShapeDtypeStruct((1, CORES * count, panel), mine[0].dtype)] * 2,
+        in_specs=[vmem] * (2 * len(mine)),
+        out_specs=[vmem] * 2,
         compiler_params=pltpu.CompilerParams(vmem_limit_bytes=SMALL_GRANT),
         name="join",
-    )(mine, theirs)
+    )(*mine, *theirs)
 
 
 def run_first(batches, distances, others, row_masks, field, orders):
@@ -323,7 +321,7 @@
     return pl.pallas_call(
         functools.partial(cascade_first_kernel, distances, row_masks),
         out_shape=[
-            jax.ShapeDtypeStruct((2, count, panel), jnp.float32),
+            jax.ShapeDtypeStruct((count, panel), jnp.float32),
             window,
             window,
             jax.ShapeDtypeStruct((GROUP, LANES), jnp.int32),
@@ -341,19 +339,19 @@
     )(*batches, *others, field)
 
 
-def run_next(step, groups, upper, lower, starts, field, kept):
-    vmem = pl.BlockSpec(memory_space=pltpu.VMEM)
-    out_shape = [jax.ShapeDtypeStruct(kept.shape, jnp.float32)]
+def run_next(step, groups, upper, lower, starts, field, panel):
+    vmem = pl.BlockSpec(memory_space=pltpu.VMEM)
+    out_shape = [jax.ShapeDtypeStruct((field.shape[0], panel), jnp.float32)]
     if step < groups - 1:
         out_shape.append(jax.ShapeDtypeStruct(field.shape, jnp.bfloat16))
     return pl.pallas_call(
         functools.partial(cascade_next_kernel, step, groups),
         out_shape=out_shape,
-        in_specs=[vmem] * 5,
+        in_specs=[vmem] * 4,
         out_specs=[vmem] * len(out_shape),
         compiler_params=pltpu.CompilerParams(vmem_limit_bytes=24 * 1024 * 1024),
         name=f"cascade_{step}",
-    )(upper, lower, starts, field, kept)
+    )(upper, lower, starts, field)
 
 
 def gather_batches(own, corner, across, rows):
@@ -417,9 +415,10 @@
     for mask in range(1, rows - 1):
         others.append(across(whole, ((0, mask), (0, mask))))
         row_masks.append(mask)
-    kept, upper, lower, starts, send = run_first(
+    mine, upper, lower, starts, send = run_first(
         batches, distances, others, tuple(row_masks), field, orders
     )
+    results = []
     for step in range(1, groups):
         pairs = []
         for index in range(GROUP * rows):
@@ -428,9 +427,13 @@
             pairs.append((forward_from, forward_from + GROUP * rows))
             pairs.append((adjoint_from, adjoint_from - GROUP * rows))
         field = lax.ppermute(send, ("layer", "row"), pairs)
-        kept, *send = run_next(step, groups, upper, lower, starts, field, kept)
+        theirs = across(mine, ((1, 0), (1, 0)))
+        field, theirs = lax.optimization_barrier((field, theirs))
+        results.append((mine, theirs))
+        mine, *send = run_next(step, groups, upper, lower, starts, field, panel)
         send = send[0] if send else None
-    return tuple(join(kept, across(kept, ((1, 0), (1, 0)))))
+    results.append((mine, across(mine, ((1, 0), (1, 0)))))
+    return tuple(join(*zip(*results)))
 
 
 def solution(mesh):

time: 45.3 us -> 45.3 us (level)
    ppermute x10 -> x11, waiting for transfers between devices: 7.14 us -> 7.1 us  [across(): return lax.ppermute(array, ('layer', 'row'), pairs)]
    ppermute x10 -> x11, starting transfers between devices: 10.8 us -> 10.8 us  [across(): return lax.ppermute(array, ('layer', 'row'), pairs)]
  transfers between devices with their start and end apart: 11 -> 12, of which waited for: 7 -> 7; matrix products, arithmetic and copies ran while one was open for 2% -> 2% of each run, Pallas kernels for 0% -> 0%
where the time goes in v3:
time: 45.3 us; the launch traced here: 45 us
  Pallas kernels  18.1 us (40%)
  starting transfers between devices  13.5 us (30%)
  waiting for transfers between devices  9.4 us (21%)
  between operations  2 us (4%)
  local copies, waits for them, and re-layouts  1.22 us (3%)
  other arithmetic  0.78 us (2%)
    ppermute x11, starting transfers between devices, across(): return lax.ppermute(array, ('layer', 'row'), pairs)  10.8 us
    pallas_call x1, Pallas kernels, run_first(): pl.pallas_call(functools.partial(cascade_first_kernel, distances, row_mas...  8.85 us
    pallas_call x1, Pallas kernels, run_next(): pl.pallas_call(functools.partial(cascade_next_kernel, step, groups), out_...  8.19 us
    ppermute x11, waiting for transfers between devices, across(): return lax.ppermute(array, ('layer', 'row'), pairs)  7.1 us
    ppermute x1, starting transfers between devices, on_device(): field = lax.ppermute(send, ('layer', 'row'), pairs)  2.65 us
    ppermute x1, waiting for transfers between devices, on_device(): field = lax.ppermute(send, ('layer', 'row'), pairs)  2.3 us
    unnamed x2, local copies, waits for them, and re-layouts  1.22 us
  transfers between devices with their start and end apart: 12, of which 7 were waited for; matrix products, arithmetic and copies ran while one was open for 2% of the time, Pallas kernels for 0%

profile of v3, /device:TPU:0, one launch (start us, length us, event | category | flops | bytes accessed | tf_op | source)
XLA Modules:
  0.0 45.0 jit_solution(11214200090681510647)
XLA Ops:
  1.9 1.2 %copy-done = bf16[1,512,1024]{2,1,0:T(8,128)(2,1)S(1)} copy-done((bf16[1,512,1024]{2,1,0:T(8,128)(2,1)S(1)}, bf16[1,512,1024]{2,1,0:T(8,128)(2,1)}, u32[]{:S(2)}) %copy-start) | copy-done | bytes 1048600
  3.1 0.3 fold.1.refs_0_.folded
  3.5 3.1 %collective-permute-start.2 = (bf16[448,128]{1,0:T(8,128)(2,1)S(1)}, bf16[448,128]{1,0:T(8,128)(2,1)S(1)}, u32[]{:S(2)}, u32[]{:S(2)}) collective-permute-start(bf16[448,128]{1,0:T(8,128)(2,1)S(1)} %fold.1.refs_0_.folded), channel_id=1, source_target_pairs={{0,8},{1,9},{2,3},{3,2},{4,12},{5,13},{6,7},{7,6},{8,0},{9,1},{10,... | collective-permute-start | bytes 344072 | tf_op jit(solution)/shard_map/ppermute | solution.py:404
  6.6 1.5 %collective-permute-start.1 = (bf16[448,128]{1,0:T(8,128)(2,1)S(1)}, bf16[448,128]{1,0:T(8,128)(2,1)S(1)}, u32[]{:S(2)}, u32[]{:S(2)}) collective-permute-start(bf16[448,128]{1,0:T(8,128)(2,1)S(1)} %fold.1.refs_0_.folded), channel_id=1, source_target_pairs={{0,4},{1,5},{2,10},{3,11},{4,0},{5,1},{6,14},{7,15},{8,12},{9,13},... | collective-permute-start | bytes 344072 | tf_op jit(solution)/shard_map/ppermute | solution.py:404
  8.1 1.5 %collective-permute-start = (bf16[448,128]{1,0:T(8,128)(2,1)S(1)}, bf16[448,128]{1,0:T(8,128)(2,1)S(1)}, u32[]{:S(2)}, u32[]{:S(2)}) collective-permute-start(bf16[448,128]{1,0:T(8,128)(2,1)S(1)} %fold.1.refs_0_.folded), channel_id=1, source_target_pairs={{0,1},{1,0},{2,6},{3,7},{4,5},{5,4},{6,2},{7,3},{8,9},{9,8},{10,14... | collective-permute-start | bytes 344072 | tf_op jit(solution)/shard_map/ppermute | solution.py:404
  9.6 0.8 %dynamic-slice_select_fusion.field.refs_5_ = f32[16,512]{1,0:T(8,128)S(1)} fusion(f32[32,512]{1,0:T(8,128)} %param.9, s32[]{:T(128)S(6)} %select_n.26, f32[32,512]{1,0:T(8,128)} %param.8, pred[]{:T(512)S(6)} %eq.5), kind=kLoop, calls=%fused_computation | loop fusion | flops 8192 | bytes 98309 | tf_op jit(solution)/shard_map/jit(_where)/select_n | solution.py:410
  10.4 0.1 collective-permute-start.7
  10.5 1.9 %collective-permute-start.6 = (bf16[448,128]{1,0:T(8,128)(2,1)S(1)}, bf16[448,128]{1,0:T(8,128)(2,1)S(1)}, u32[]{:S(2)}, u32[]{:S(2)}) collective-permute-start(bf16[448,128]{1,0:T(8,128)(2,1)S(1)} %collective-permute-done.2.refs_3_), channel_id=1, source_target_pairs={{0,4},{1,5},{2,10},{3,11},{4,0},{5,1},{6,14},{7,15},{8,12},{9,13},... | collective-permute-start | bytes 344072 | tf_op jit(solution)/shard_map/ppermute | solution.py:404
  12.4 0.5 %collective-permute-done.1.refs_2_ = bf16[448,128]{1,0:T(8,128)(2,1)S(1)} collective-permute-done((bf16[448,128]{1,0:T(8,128)(2,1)S(1)}, bf16[448,128]{1,0:T(8,128)(2,1)S(1)}, u32[]{:S(2)}, u32[]{:S(2)}) %collective-permute-start.1) | collective-permute-done | bytes 114720 | tf_op jit(solution)/shard_map/ppermute | solution.py:404
  12.9 1.0 %collective-permute-start.4 = (bf16[448,128]{1,0:T(8,128)(2,1)S(1)}, bf16[448,128]{1,0:T(8,128)(2,1)S(1)}, u32[]{:S(2)}, u32[]{:S(2)}) collective-permute-start(bf16[448,128]{1,0:T(8,128)(2,1)S(1)} %collective-permute-done.1.refs_2_), channel_id=1, source_target_pairs={{0,1},{1,0},{2,6},{3,7},{4,5},{5,4},{6,2},{7,3},{8,9},{9,8},{10,14... | collective-permute-start | bytes 344072 | tf_op jit(solution)/shard_map/ppermute | solution.py:404
  13.8 1.6 %collective-permute-start.5 = (bf16[448,128]{1,0:T(8,128)(2,1)S(1)}, bf16[448,128]{1,0:T(8,128)(2,1)S(1)}, u32[]{:S(2)}, u32[]{:S(2)}) collective-permute-start(bf16[448,128]{1,0:T(8,128)(2,1)S(1)} %collective-permute-done.refs_1_), channel_id=1, source_target_pairs={{0,8},{1,9},{2,3},{3,2},{4,12},{5,13},{6,7},{7,6},{8,0},{9,1},{10,... | collective-permute-start | bytes 344072 | tf_op jit(solution)/shard_map/ppermute | solution.py:404
  15.4 0.1 collective-permute-start.3
  15.5 2.5 %collective-permute-done.7.refs_3_.refs_4_ = bf16[512,128]{1,0:T(8,128)(2,1)S(1)} collective-permute-done((bf16[512,128]{1,0:T(8,128)(2,1)S(1)}, bf16[512,128]{1,0:T(8,128)(2,1)S(1)}, u32[]{:S(2)}, u32[]{:S(2)}) %collective-permute-start.7) | collective-permute-done | bytes 131104 | tf_op jit(solution)/shard_map/ppermute | solution.py:404
  18.0 0.1 collective-permute-done.6.refs_2_
  18.1 1.0 %collective-permute-done.4.refs_0_ = bf16[448,128]{1,0:T(8,128)(2,1)S(1)} collective-permute-done((bf16[448,128]{1,0:T(8,128)(2,1)S(1)}, bf16[448,128]{1,0:T(8,128)(2,1)S(1)}, u32[]{:S(2)}, u32[]{:S(2)}) %collective-permute-start.4) | collective-permute-done | bytes 114720 | tf_op jit(solution)/shard_map/ppermute | solution.py:404
  19.2 0.1 collective-permute-start.8
  19.3 1.8 %collective-permute-done.8.refs_3_ = bf16[4,448,128]{2,1,0:T(8,128)(2,1)S(1)} collective-permute-done((bf16[4,448,128]{2,1,0:T(8,128)(2,1)S(1)}, bf16[4,448,128]{2,1,0:T(8,128)(2,1)S(1)}, u32[]{:S(2)}, u32[]{:S(2)}) %collective-permute-start.8) | collective-permute-done | bytes 458784 | tf_op jit(solution)/shard_map/ppermute | solution.py:404
  21.1 8.9 %cascade_first.1 = (f32[16,512]{1,0:T(8,128)S(1)}, bf16[8,8,128,256]{3,2,1,0:T(8,128)(2,1)S(1)}, bf16[8,8,128,256]{3,2,1,0:T(8,128)(2,1)S(1)}, s32[8,128]{1,0:T(8,128)S(1)}, bf16[16,1024]{1,0:T(8,128)(2,1)S(1)}) custom-call(bf16[4,448,128]{2,1,0:T(8,128)(2,1)S(1)} %batch.2.refs_0_, bf16[4,448,128]{2,1,0:T(8,128)(2,1)S(1)} %collective-permute-done.3.refs_1_, ...), custom_call_target="tpu_custom_call" | custom-call | tf_op jit(solution)/shard_map/cascade_first/pallas_call | solution.py:321
  29.9 2.7 %collective-permute-start.9 = (bf16[16,1024]{1,0:T(8,128)(2,1)S(1)}, bf16[16,1024]{1,0:T(8,128)(2,1)S(1)}, u32[]{:S(2)}, u32[]{:S(2)}) collective-permute-start(bf16[16,1024]{1,0:T(8,128)(2,1)S(1)} %get-tuple-element.19), channel_id=1, source_target_pairs={{0,16},{16,0},{1,17},{17,1},{2,18},{18,2},{3,19},{19,3},{4,20},{20... | collective-permute-start | bytes 98312 | tf_op jit(solution)/shard_map/ppermute | solution.py:429
  32.6 2.3 %collective-permute-done.9.refs_3_ = bf16[16,1024]{1,0:T(8,128)(2,1)S(1)} collective-permute-done((bf16[16,1024]{1,0:T(8,128)(2,1)S(1)}, bf16[16,1024]{1,0:T(8,128)(2,1)S(1)}, u32[]{:S(2)}, u32[]{:S(2)}) %collective-permute-start.9) | collective-permute-done | bytes 32800 | tf_op jit(solution)/shard_map/ppermute | solution.py:429
  34.9 8.2 %cascade_1.1.refs_1_ = f32[16,512]{1,0:T(8,128)S(1)} custom-call(bf16[8,8,128,256]{3,2,1,0:T(8,128)(2,1)S(1)} %get-tuple-element.16.refs_0_, bf16[8,8,128,256]{3,2,1,0:T(8,128)(2,1)S(1)} %get-tuple-element.17.refs_1_, s32[8,128]{1,0:T(8,128)S(1)} %get-tuple-element.18.refs_2_, bf16[16,1024]{1,0:T(8,128)(2,1)S(1)} %collective-permute-done.9.refs_3_), custom_call_target="tpu_custom_call" | custom-call | tf_op jit(solution)/shard_map/cascade_1/pallas_call | solution.py:347
  43.1 0.1 collective-permute-start.11
  43.1 1.2 %collective-permute-done.11.refs_3_ = f32[16,512]{1,0:T(8,128)S(1)} collective-permute-done((f32[16,512]{1,0:T(8,128)S(1)}, f32[16,512]{1,0:T(8,128)S(1)}, u32[]{:S(2)}, u32[]{:S(2)}) %collective-permute-start.11) | collective-permute-done | bytes 32800 | tf_op jit(solution)/shard_map/ppermute | solution.py:404
  44.3 0.7 %join.1 = (f32[1,32,512]{2,1,0:T(8,128)}, f32[1,32,512]{2,1,0:T(8,128)}) custom-call(f32[16,512]{1,0:T(8,128)S(1)} %get-tuple-element.15.refs_0_, f32[16,512]{1,0:T(8,128)S(1)} %cascade_1.1.refs_1_, f32[16,512]{1,0:T(8,128)S(1)} %collective-permute-done.10.refs_2_, f32[16,512]{1,0:T(8,128)S(1)} %collective-permute-done.11.refs_3_), custom_call_target="tpu_custom_call" | custom-call | tf_op jit(solution)/shard_map/join/pallas_call | solution.py:306
  (10 shorter events, 0.1 us)
Async XLA Ops:
  1.9 1.2 %copy-start = (bf16[1,512,1024]{2,1,0:T(8,128)(2,1)S(1)}, bf16[1,512,1024]{2,1,0:T(8,128)(2,1)}, u32[]{:S(2)}) copy-start(bf16[1,512,1024]{2,1,0:T(8,128)(2,1)} %coupling_ref.1) | copy-start | bytes 3145732
  3.5 7.0 %collective-permute-start.2 = (bf16[448,128]{1,0:T(8,128)(2,1)S(1)}, bf16[448,128]{1,0:T(8,128)(2,1)S(1)}, u32[]{:S(2)}, u32[]{:S(2)}) collective-permute-start(bf16[448,128]{1,0:T(8,128)(2,1)S(1)} %fold.1.refs_0_.folded), channel_id=1, source_target_pairs={{0,8},{1,9},{2,3},{3,2},{4,12},{5,13},{6,7},{7,6},{8,0},{9,1},{10,... | collective-permute-start | bytes 344072 | tf_op jit(solution)/shard_map/ppermute | solution.py:404
  6.6 6.3 %collective-permute-start.1 = (bf16[448,128]{1,0:T(8,128)(2,1)S(1)}, bf16[448,128]{1,0:T(8,128)(2,1)S(1)}, u32[]{:S(2)}, u32[]{:S(2)}) collective-permute-start(bf16[448,128]{1,0:T(8,128)(2,1)S(1)} %fold.1.refs_0_.folded), channel_id=1, source_target_pairs={{0,4},{1,5},{2,10},{3,11},{4,0},{5,1},{6,14},{7,15},{8,12},{9,13},... | collective-permute-start | bytes 344072 | tf_op jit(solution)/shard_map/ppermute | solution.py:404
  8.1 5.8 %collective-permute-start = (bf16[448,128]{1,0:T(8,128)(2,1)S(1)}, bf16[448,128]{1,0:T(8,128)(2,1)S(1)}, u32[]{:S(2)}, u32[]{:S(2)}) collective-permute-start(bf16[448,128]{1,0:T(8,128)(2,1)S(1)} %fold.1.refs_0_.folded), channel_id=1, source_target_pairs={{0,1},{1,0},{2,6},{3,7},{4,5},{5,4},{6,2},{7,3},{8,9},{9,8},{10,14... | collective-permute-start | bytes 344072 | tf_op jit(solution)/shard_map/ppermute | solution.py:404
  10.4 7.6 %collective-permute-start.7 = (bf16[512,128]{1,0:T(8,128)(2,1)S(1)}, bf16[512,128]{1,0:T(8,128)(2,1)S(1)}, u32[]{:S(2)}, u32[]{:S(2)}) collective-permute-start(bf16[512,128]{1,0:T(8,128)(2,1)S(1)} %corner.1), channel_id=1, source_target_pairs={{0,13},{1,12},{2,15},{3,14},{4,9},{5,8},{6,11},{7,10},{8,5},{9,4},... | collective-permute-start | bytes 393224 | tf_op jit(solution)/shard_map/ppermute | solution.py:404
  10.5 7.7 %collective-permute-start.6 = (bf16[448,128]{1,0:T(8,128)(2,1)S(1)}, bf16[448,128]{1,0:T(8,128)(2,1)S(1)}, u32[]{:S(2)}, u32[]{:S(2)}) collective-permute-start(bf16[448,128]{1,0:T(8,128)(2,1)S(1)} %collective-permute-done.2.refs_3_), channel_id=1, source_target_pairs={{0,4},{1,5},{2,10},{3,11},{4,0},{5,1},{6,14},{7,15},{8,12},{9,13},... | collective-permute-start | bytes 344072 | tf_op jit(solution)/shard_map/ppermute | solution.py:404
  12.9 6.3 %collective-permute-start.4 = (bf16[448,128]{1,0:T(8,128)(2,1)S(1)}, bf16[448,128]{1,0:T(8,128)(2,1)S(1)}, u32[]{:S(2)}, u32[]{:S(2)}) collective-permute-start(bf16[448,128]{1,0:T(8,128)(2,1)S(1)} %collective-permute-done.1.refs_2_), channel_id=1, source_target_pairs={{0,1},{1,0},{2,6},{3,7},{4,5},{5,4},{6,2},{7,3},{8,9},{9,8},{10,14... | collective-permute-start | bytes 344072 | tf_op jit(solution)/shard_map/ppermute | solution.py:404
  13.8 5.3 %collective-permute-start.5 = (bf16[448,128]{1,0:T(8,128)(2,1)S(1)}, bf16[448,128]{1,0:T(8,128)(2,1)S(1)}, u32[]{:S(2)}, u32[]{:S(2)}) collective-permute-start(bf16[448,128]{1,0:T(8,128)(2,1)S(1)} %collective-permute-done.refs_1_), channel_id=1, source_target_pairs={{0,8},{1,9},{2,3},{3,2},{4,12},{5,13},{6,7},{7,6},{8,0},{9,1},{10,... | collective-permute-start | bytes 344072 | tf_op jit(solution)/shard_map/ppermute | solution.py:404
  15.4 3.8 %collective-permute-start.3 = (bf16[4,448,128]{2,1,0:T(8,128)(2,1)S(1)}, bf16[4,448,128]{2,1,0:T(8,128)(2,1)S(1)}, u32[]{:S(2)}, u32[]{:S(2)}) collective-permute-start(bf16[4,448,128]{2,1,0:T(8,128)(2,1)S(1)} %batch.2.refs_0_), channel_id=1, source_target_pairs={{0,2},{1,3},{2,0},{3,1},{4,6},{5,7},{6,4},{7,5},{8,10},{9,11},{10,... | collective-permute-start | bytes 1376264 | tf_op jit(solution)/shard_map/ppermute | solution.py:404
  19.2 1.9 %collective-permute-start.8 = (bf16[4,448,128]{2,1,0:T(8,128)(2,1)S(1)}, bf16[4,448,128]{2,1,0:T(8,128)(2,1)S(1)}, u32[]{:S(2)}, u32[]{:S(2)}) collective-permute-start(bf16[4,448,128]{2,1,0:T(8,128)(2,1)S(1)} %batch.3.refs_2_), channel_id=1, source_target_pairs={{0,2},{1,3},{2,0},{3,1},{4,6},{5,7},{6,4},{7,5},{8,10},{9,11},{10,... | collective-permute-start | bytes 1376264 | tf_op jit(solution)/shard_map/ppermute | solution.py:404
  29.9 5.0 %collective-permute-start.9 = (bf16[16,1024]{1,0:T(8,128)(2,1)S(1)}, bf16[16,1024]{1,0:T(8,128)(2,1)S(1)}, u32[]{:S(2)}, u32[]{:S(2)}) collective-permute-start(bf16[16,1024]{1,0:T(8,128)(2,1)S(1)} %get-tuple-element.19), channel_id=1, source_target_pairs={{0,16},{16,0},{1,17},{17,1},{2,18},{18,2},{3,19},{19,3},{4,20},{20... | collective-permute-start | bytes 98312 | tf_op jit(solution)/shard_map/ppermute | solution.py:429
  32.6 2.3 %collective-permute-start.10 = (f32[16,512]{1,0:T(8,128)S(1)}, f32[16,512]{1,0:T(8,128)S(1)}, u32[]{:S(2)}, u32[]{:S(2)}) collective-permute-start(f32[16,512]{1,0:T(8,128)S(1)} %get-tuple-element.15.refs_0_), channel_id=1, source_target_pairs={{0,2},{1,3},{2,0},{3,1},{4,6},{5,7},{6,4},{7,5},{8,10},{9,11},{10,... | collective-permute-start | bytes 98312 | tf_op jit(solution)/shard_map/ppermute | solution.py:404
  43.1 1.3 %collective-permute-start.11 = (f32[16,512]{1,0:T(8,128)S(1)}, f32[16,512]{1,0:T(8,128)S(1)}, u32[]{:S(2)}, u32[]{:S(2)}) collective-permute-start(f32[16,512]{1,0:T(8,128)S(1)} %cascade_1.1.refs_1_), channel_id=1, source_target_pairs={{0,2},{1,3},{2,0},{3,1},{4,6},{5,7},{6,4},{7,5},{8,10},{9,11},{10,... | collective-permute-start | bytes 98312 | tf_op jit(solution)/shard_map/ppermute | solution.py:404
